TPU v7x, 32 devices: a whole 2x2x4 slice. The times are simulated.
32 devices in a mesh: groups: 2 (over x), blk: 16 (over z, y, core).
Axes of the slice: x: 2, y: 2, z: 4, core: 2. Of those that a mesh axis runs over, the one named last changes fastest.
Arguments:
- queries: bfloat16 [4096, 512], P(('groups', 'blk')), parts along dimension 0, may hold values from -8 to 8
- key_states: bfloat16 [4096, 128], P(('groups', 'blk')), parts along dimension 0, may hold values from -6 to 6
- value_states: bfloat16 [4096, 128], P(('groups', 'blk')), parts along dimension 0, may hold values from -6 to 6
- grad_out: bfloat16 [4096, 512], P(('groups', 'blk')), parts along dimension 0, may hold values from -6 to 6
- tile_mask: int32 [32, 16], P('groups'), parts along dimension 0, may hold values 0 or 1
- block_order: int32 [32], P('groups'), parts along dimension 0, may hold values from 0 to 15, each once
Outputs:
- attended: bfloat16 [4096, 512], P(('groups', 'blk')), parts along dimension 0
- grad_queries: bfloat16 [4096, 512], P(('groups', 'blk')), parts along dimension 0
- grad_keys: float32 [4096, 128], P(('groups', 'blk')), parts along dimension 0
- grad_values: float32 [4096, 128], P(('groups', 'blk')), parts along dimension 0
There are 2 independent parts, one for each index of `groups`. A program takes and returns all parts, laid end to end along the dimension named above; each array names one. Nothing has to cross between parts.
Inputs may be any that keep to these rules, and one draw needn't show every extreme that they name: `block_order`: each block number appears once.
All inputs are finite; a program needn't handle non-finite values.
Results may differ from a plain program's by a relative error of at most 0.04.
Values may be sent and summed in bfloat16 or wider, within the bound.
A program may use at most 64 MiB of HBM per device.

v0:
```python
import jax
import jax.numpy as jnp
from jax import lax
from jax.sharding import PartitionSpec as P

TILE = 128


def passed_along(value, axis, steps):
    count = lax.axis_size(axis)
    pairs = [(source, (source + steps) % count) for source in range(count)]
    return lax.ppermute(value, axis, pairs)


def shards(queries, key_states, value_states, grad_out, tile_mask, block_order):
    cycle_size = lax.axis_size("blk")
    my_index = lax.axis_index("blk")
    tok_rows = key_states.shape[0]
    head_width = key_states.shape[1]
    head_count = queries.shape[1] // head_width
    scaling = head_width ** (-0.5)
    tiles_per = tok_rows // TILE
    tile_total = tile_mask.shape[1]
    offsets = jnp.arange(tok_rows, dtype=jnp.int32)
    my_block = block_order[my_index]
    total_rows = head_count * tok_rows

    def to_rows(features):
        return (
            features.reshape(tok_rows, head_count, head_width)
            .transpose(1, 0, 2)
            .reshape(total_rows, head_width)
        )

    def from_rows(row_form):
        return (
            row_form.reshape(head_count, tok_rows, head_width)
            .transpose(1, 0, 2)
            .reshape(tok_rows, head_count * head_width)
        )

    query_rows = to_rows(queries)
    cot_rows = to_rows(grad_out)

    def mask_for(query_block, key_pos):
        query_pos = query_block * tok_rows + offsets
        tile_rows = lax.dynamic_slice_in_dim(
            tile_mask, query_block * tiles_per, tiles_per, 0
        ).astype(jnp.float32)
        tile_rows = jnp.repeat(tile_rows, TILE, axis=0)
        one_hot = (
            (key_pos // TILE)[:, None] == jnp.arange(tile_total, dtype=jnp.int32)[None, :]
        ).astype(jnp.float32)
        tile_bits = jnp.dot(tile_rows, one_hot.T, preferred_element_type=jnp.float32) > 0.5
        same_tile = (query_pos // TILE)[:, None] == (key_pos // TILE)[None, :]
        allowed = (query_pos[:, None] >= key_pos[None, :]) & (tile_bits | same_tile)
        return jnp.tile(allowed, (head_count, 1))

    def softmax_update(carry_state, key_sub, value_sub, allowed):
        run_max, run_sum, run_acc = carry_state
        scores = (
            jnp.einsum("rd,kd->rk", query_rows, key_sub, preferred_element_type=jnp.float32)
            * scaling
        )
        scores = jnp.where(allowed, scores, -1e30)
        new_max = jnp.maximum(run_max, jnp.max(scores, axis=1))
        weights = jnp.where(allowed, jnp.exp(scores - new_max[:, None]), 0.0)
        factor = jnp.exp(run_max - new_max)
        run_sum = run_sum * factor + jnp.sum(weights, axis=1)
        run_acc = run_acc * factor[:, None] + jnp.dot(
            weights.astype(jnp.bfloat16), value_sub, preferred_element_type=jnp.float32
        )
        return (new_max, run_sum, run_acc)

    def guarded_update(carry_state, key_sub, value_sub, allowed):
        return softmax_update(carry_state, key_sub, value_sub, allowed)

    start_state = (
        jnp.full((total_rows,), -1e30, jnp.float32),
        jnp.zeros((total_rows,), jnp.float32),
        jnp.zeros((total_rows, head_width), jnp.float32),
    )
    key_piece = lax.all_gather(key_states, "blk", axis=0, tiled=True)
    value_piece = lax.all_gather(value_states, "blk", axis=0, tiled=True)
    piece_rows = key_piece.shape[0]

    def sub_step(sub_num, inner_state):
        first = sub_num * tok_rows
        key_sub = lax.dynamic_slice_in_dim(key_piece, first, tok_rows, 0)
        value_sub = lax.dynamic_slice_in_dim(value_piece, first, tok_rows, 0)
        key_ids = first + jnp.arange(tok_rows, dtype=jnp.int32)
        owners = key_ids // tok_rows
        owner_blocks = jnp.sum(
            jnp.where(
                owners[:, None] == jnp.arange(cycle_size, dtype=jnp.int32)[None, :],
                block_order[None, :],
                0,
            ),
            axis=1,
        )
        key_pos = owner_blocks * tok_rows + key_ids % tok_rows
        return guarded_update(inner_state, key_sub, value_sub, mask_for(my_block, key_pos))

    run_max, run_sum, run_acc = lax.fori_loop(0, piece_rows // tok_rows, sub_step, start_state)
    log_sum = run_max + jnp.log(run_sum)
    out_rows = (run_acc / run_sum[:, None]).astype(jnp.bfloat16)
    attended = from_rows(out_rows)
    row_delta = jnp.sum(cot_rows.astype(jnp.float32) * out_rows.astype(jnp.float32), axis=1)

    def block_grads(q_part, cot_part, sum_part, delta_part, key_sub, value_sub, allowed):
        scores = (
            jnp.einsum("rd,kd->rk", q_part, key_sub, preferred_element_type=jnp.float32) * scaling
        )
        weights = jnp.where(allowed, jnp.exp(scores - sum_part[:, None]), 0.0)
        value_term = jnp.einsum(
            "rk,rd->kd", weights.astype(jnp.bfloat16), cot_part, preferred_element_type=jnp.float32
        )
        d_prob = jnp.einsum("rd,kd->rk", cot_part, value_sub, preferred_element_type=jnp.float32)
        d_score = (weights * (d_prob - delta_part[:, None])).astype(jnp.bfloat16)
        query_term = jnp.dot(d_score, key_sub, preferred_element_type=jnp.float32) * scaling
        key_term = (
            jnp.einsum("rk,rd->kd", d_score, q_part, preferred_element_type=jnp.float32) * scaling
        )
        return (query_term, key_term, value_term)

    def guarded_grads(q_part, cot_part, sum_part, delta_part, key_sub, value_sub, allowed):
        return block_grads(q_part, cot_part, sum_part, delta_part, key_sub, value_sub, allowed)

    zero_keys = jnp.zeros((tok_rows, head_width), jnp.float32)
    zero_queries = jnp.zeros((total_rows, head_width), jnp.float32)

    def key_step(step_num, carry_state):
        key_cur, value_cur, key_acc, value_acc, query_acc = carry_state
        source = (my_index - step_num) % cycle_size
        key_pos = block_order[source] * tok_rows + offsets
        allowed = mask_for(my_block, key_pos)
        query_term, key_term, value_term = guarded_grads(
            query_rows, cot_rows, log_sum, row_delta, key_cur, value_cur, allowed
        )
        return (
            key_cur,
            value_cur,
            key_acc + key_term,
            value_acc + value_term,
            query_acc + query_term,
        )

    def key_turn(step_num, carry_state):
        key_cur, value_cur, key_acc, value_acc, query_acc = key_step(step_num, carry_state)
        key_cur, value_cur = passed_along((key_cur, value_cur), "blk", 1)
        key_acc, value_acc = passed_along((key_acc, value_acc), "blk", 1)
        return (key_cur, value_cur, key_acc, value_acc, query_acc)

    carry_state = (key_states, value_states, zero_keys, zero_keys, zero_queries)
    carry_state = lax.fori_loop(0, cycle_size - 1, key_turn, carry_state)
    carry_state = key_step(cycle_size - 1, carry_state)
    key_acc, value_acc = passed_along((carry_state[2], carry_state[3]), "blk", 1)
    query_acc = carry_state[4]
    grad_queries = from_rows(query_acc.astype(jnp.bfloat16))
    return (attended, grad_queries, key_acc, value_acc)


def solution(mesh):
    placed = (
        P(("groups", "blk"), None),
        P(("groups", "blk"), None),
        P(("groups", "blk"), None),
        P(("groups", "blk"), None),
        P("groups", None),
        P("groups"),
    )
    return jax.shard_map(
        shards,
        mesh=mesh,
        in_specs=placed,
        out_specs=(
            P(("groups", "blk"), None),
            P(("groups", "blk"), None),
            P(("groups", "blk"), None),
            P(("groups", "blk"), None),
        ),
        check_vma=False,
    )
```

profile of v0, /device:TPU:0, one launch (start us, length us, event | category | flops | bytes accessed | tf_op | source)
XLA Modules:
  0.0 222.9 jit_solution(3966216597943441637)
XLA Ops:
  0.7 0.8 copy.83
  1.5 0.7 copy-done.3
  4.7 0.7 dynamic-slice_convert_fusion
  5.4 0.7 fusion.73
  6.8 24.6 %all_gather.6 = bf16[2048,128]{1,0:T(8,128)(2,1)S(1)} all-gather(bf16[128,128]{1,0:T(8,128)(2,1)S(1)} %copy.83), channel_id=1, replica_groups=mesh['groups'=2,'blk'=16] {'blk'}, dimensions={0}, use_global_device_ids=true | all-gather | bytes 557056 | tf_op jit(solution)/shard_map/all_gather | solution.py:83
  31.4 18.9 %all_gather.7 = bf16[2048,128]{1,0:T(8,128)(2,1)S(1)} all-gather(bf16[128,128]{1,0:T(8,128)(2,1)S(1)} %copy.84), channel_id=1, replica_groups=mesh['groups'=2,'blk'=16] {'blk'}, dimensions={0}, use_global_device_ids=true | all-gather | bytes 557056 | tf_op jit(solution)/shard_map/all_gather | solution.py:84
  50.2 17.7 %while.47 = (s32[]{:T(128)}, f32[512]{0:T(512)S(1)}, f32[512]{0:T(512)S(1)}, f32[512,128]{1,0:T(8,128)S(1)}, s32[]{:T(128)}, /*index=5*/s32[16]{0:T(128)S(1)}, b...) while((s32[]{:T(128)}, f32[512]{0:T(512)S(1)}, ...), condition=%wide.region_4.5_spmd.clone, body=%wide.region_0.4_spmd.clone.sunk | while | flops 34965508 | bytes 1841459 | solution.py:104
  69.2 144.8 %while.48 = (s32[]{:T(128)}, bf16[128,128]{1,0:T(8,128)(2,1)S(1)}, bf16[128,128]{1,0:T(8,128)(2,1)S(1)}, f32[128,128]{1,0:T(8,128)S(1)}, f32[128,128]{1,0:T(8,12...) while((s32[]{:T(128)}, bf16[128,128]{1,0:T(8,128)(2,1)S(1)}, ...), condition=%wide.region_7.8_spmd.clone.clone, body=%wide.region_6.7_spmd.clone.clone.sunk | while | flops 85202960 | bytes 3711538 | solution.py:155
  69.7 1.5 collective-permute-start.1
  74.4 0.9 collective-permute-done
  75.7 4.2 %collective-permute-done.2 = f32[128,128]{1,0:T(8,128)S(1)} collective-permute-done((f32[128,128]{1,0:T(8,128)S(1)}, f32[128,128]{1,0:T(8,128)S(1)}, u32[]{:S(2)}, u32[]{:S(2)}) %collective-permute-start.2) | collective-permute-done | bytes 65568 | tf_op jit(solution)/shard_map/while/body/eval_jaxpr/ppermute | solution.py:12
  79.9 0.7 collective-permute-done.3
  80.7 0.6 dynamic_slice.79
  83.6 3.1 %collective-permute-done = bf16[128,128]{1,0:T(8,128)(2,1)S(1)} collective-permute-done((bf16[128,128]{1,0:T(8,128)(2,1)S(1)}, bf16[128,128]{1,0:T(8,128)(2,1)S(1)}, u32[]{:S(2)}, u32[]{:S(2)}) %collective-permute-start) | collective-permute-done | bytes 32800 | tf_op jit(solution)/shard_map/while/body/eval_jaxpr/ppermute | solution.py:12
  87.0 2.4 %collective-permute-done.2 = f32[128,128]{1,0:T(8,128)S(1)} collective-permute-done((f32[128,128]{1,0:T(8,128)S(1)}, f32[128,128]{1,0:T(8,128)S(1)}, u32[]{:S(2)}, u32[]{:S(2)}) %collective-permute-start.2) | collective-permute-done | bytes 65568 | tf_op jit(solution)/shard_map/while/body/eval_jaxpr/ppermute | solution.py:12
  89.4 0.7 collective-permute-done.3
  90.2 0.6 dynamic_slice.79
  93.1 3.1 %collective-permute-done = bf16[128,128]{1,0:T(8,128)(2,1)S(1)} collective-permute-done((bf16[128,128]{1,0:T(8,128)(2,1)S(1)}, bf16[128,128]{1,0:T(8,128)(2,1)S(1)}, u32[]{:S(2)}, u32[]{:S(2)}) %collective-permute-start) | collective-permute-done | bytes 32800 | tf_op jit(solution)/shard_map/while/body/eval_jaxpr/ppermute | solution.py:12
  96.5 2.4 %collective-permute-done.2 = f32[128,128]{1,0:T(8,128)S(1)} collective-permute-done((f32[128,128]{1,0:T(8,128)S(1)}, f32[128,128]{1,0:T(8,128)S(1)}, u32[]{:S(2)}, u32[]{:S(2)}) %collective-permute-start.2) | collective-permute-done | bytes 65568 | tf_op jit(solution)/shard_map/while/body/eval_jaxpr/ppermute | solution.py:12
  98.9 0.7 collective-permute-done.3
  102.6 3.1 %collective-permute-done = bf16[128,128]{1,0:T(8,128)(2,1)S(1)} collective-permute-done((bf16[128,128]{1,0:T(8,128)(2,1)S(1)}, bf16[128,128]{1,0:T(8,128)(2,1)S(1)}, u32[]{:S(2)}, u32[]{:S(2)}) %collective-permute-start) | collective-permute-done | bytes 32800 | tf_op jit(solution)/shard_map/while/body/eval_jaxpr/ppermute | solution.py:12
  106.0 2.4 %collective-permute-done.2 = f32[128,128]{1,0:T(8,128)S(1)} collective-permute-done((f32[128,128]{1,0:T(8,128)S(1)}, f32[128,128]{1,0:T(8,128)S(1)}, u32[]{:S(2)}, u32[]{:S(2)}) %collective-permute-start.2) | collective-permute-done | bytes 65568 | tf_op jit(solution)/shard_map/while/body/eval_jaxpr/ppermute | solution.py:12
  108.5 0.7 collective-permute-done.3
  109.3 0.6 dynamic_slice.79
  112.2 3.1 %collective-permute-done = bf16[128,128]{1,0:T(8,128)(2,1)S(1)} collective-permute-done((bf16[128,128]{1,0:T(8,128)(2,1)S(1)}, bf16[128,128]{1,0:T(8,128)(2,1)S(1)}, u32[]{:S(2)}, u32[]{:S(2)}) %collective-permute-start) | collective-permute-done | bytes 32800 | tf_op jit(solution)/shard_map/while/body/eval_jaxpr/ppermute | solution.py:12
  115.6 2.4 %collective-permute-done.2 = f32[128,128]{1,0:T(8,128)S(1)} collective-permute-done((f32[128,128]{1,0:T(8,128)S(1)}, f32[128,128]{1,0:T(8,128)S(1)}, u32[]{:S(2)}, u32[]{:S(2)}) %collective-permute-start.2) | collective-permute-done | bytes 65568 | tf_op jit(solution)/shard_map/while/body/eval_jaxpr/ppermute | solution.py:12
  118.0 0.7 collective-permute-done.3
  121.7 3.1 %collective-permute-done = bf16[128,128]{1,0:T(8,128)(2,1)S(1)} collective-permute-done((bf16[128,128]{1,0:T(8,128)(2,1)S(1)}, bf16[128,128]{1,0:T(8,128)(2,1)S(1)}, u32[]{:S(2)}, u32[]{:S(2)}) %collective-permute-start) | collective-permute-done | bytes 32800 | tf_op jit(solution)/shard_map/while/body/eval_jaxpr/ppermute | solution.py:12
  125.1 2.4 %collective-permute-done.2 = f32[128,128]{1,0:T(8,128)S(1)} collective-permute-done((f32[128,128]{1,0:T(8,128)S(1)}, f32[128,128]{1,0:T(8,128)S(1)}, u32[]{:S(2)}, u32[]{:S(2)}) %collective-permute-start.2) | collective-permute-done | bytes 65568 | tf_op jit(solution)/shard_map/while/body/eval_jaxpr/ppermute | solution.py:12
  127.5 0.7 collective-permute-done.3
  131.2 3.1 %collective-permute-done = bf16[128,128]{1,0:T(8,128)(2,1)S(1)} collective-permute-done((bf16[128,128]{1,0:T(8,128)(2,1)S(1)}, bf16[128,128]{1,0:T(8,128)(2,1)S(1)}, u32[]{:S(2)}, u32[]{:S(2)}) %collective-permute-start) | collective-permute-done | bytes 32800 | tf_op jit(solution)/shard_map/while/body/eval_jaxpr/ppermute | solution.py:12
  134.6 2.4 %collective-permute-done.2 = f32[128,128]{1,0:T(8,128)S(1)} collective-permute-done((f32[128,128]{1,0:T(8,128)S(1)}, f32[128,128]{1,0:T(8,128)S(1)}, u32[]{:S(2)}, u32[]{:S(2)}) %collective-permute-start.2) | collective-permute-done | bytes 65568 | tf_op jit(solution)/shard_map/while/body/eval_jaxpr/ppermute | solution.py:12
  137.1 0.7 collective-permute-done.3
  140.8 3.1 %collective-permute-done = bf16[128,128]{1,0:T(8,128)(2,1)S(1)} collective-permute-done((bf16[128,128]{1,0:T(8,128)(2,1)S(1)}, bf16[128,128]{1,0:T(8,128)(2,1)S(1)}, u32[]{:S(2)}, u32[]{:S(2)}) %collective-permute-start) | collective-permute-done | bytes 32800 | tf_op jit(solution)/shard_map/while/body/eval_jaxpr/ppermute | solution.py:12
  144.2 2.4 %collective-permute-done.2 = f32[128,128]{1,0:T(8,128)S(1)} collective-permute-done((f32[128,128]{1,0:T(8,128)S(1)}, f32[128,128]{1,0:T(8,128)S(1)}, u32[]{:S(2)}, u32[]{:S(2)}) %collective-permute-start.2) | collective-permute-done | bytes 65568 | tf_op jit(solution)/shard_map/while/body/eval_jaxpr/ppermute | solution.py:12
  146.6 0.7 collective-permute-done.3
  150.3 3.1 %collective-permute-done = bf16[128,128]{1,0:T(8,128)(2,1)S(1)} collective-permute-done((bf16[128,128]{1,0:T(8,128)(2,1)S(1)}, bf16[128,128]{1,0:T(8,128)(2,1)S(1)}, u32[]{:S(2)}, u32[]{:S(2)}) %collective-permute-start) | collective-permute-done | bytes 32800 | tf_op jit(solution)/shard_map/while/body/eval_jaxpr/ppermute | solution.py:12
  153.7 2.4 %collective-permute-done.2 = f32[128,128]{1,0:T(8,128)S(1)} collective-permute-done((f32[128,128]{1,0:T(8,128)S(1)}, f32[128,128]{1,0:T(8,128)S(1)}, u32[]{:S(2)}, u32[]{:S(2)}) %collective-permute-start.2) | collective-permute-done | bytes 65568 | tf_op jit(solution)/shard_map/while/body/eval_jaxpr/ppermute | solution.py:12
  156.1 0.7 collective-permute-done.3
  159.8 3.1 %collective-permute-done = bf16[128,128]{1,0:T(8,128)(2,1)S(1)} collective-permute-done((bf16[128,128]{1,0:T(8,128)(2,1)S(1)}, bf16[128,128]{1,0:T(8,128)(2,1)S(1)}, u32[]{:S(2)}, u32[]{:S(2)}) %collective-permute-start) | collective-permute-done | bytes 32800 | tf_op jit(solution)/shard_map/while/body/eval_jaxpr/ppermute | solution.py:12
  163.2 2.4 %collective-permute-done.2 = f32[128,128]{1,0:T(8,128)S(1)} collective-permute-done((f32[128,128]{1,0:T(8,128)S(1)}, f32[128,128]{1,0:T(8,128)S(1)}, u32[]{:S(2)}, u32[]{:S(2)}) %collective-permute-start.2) | collective-permute-done | bytes 65568 | tf_op jit(solution)/shard_map/while/body/eval_jaxpr/ppermute | solution.py:12
  165.7 0.7 collective-permute-done.3
  169.4 3.1 %collective-permute-done = bf16[128,128]{1,0:T(8,128)(2,1)S(1)} collective-permute-done((bf16[128,128]{1,0:T(8,128)(2,1)S(1)}, bf16[128,128]{1,0:T(8,128)(2,1)S(1)}, u32[]{:S(2)}, u32[]{:S(2)}) %collective-permute-start) | collective-permute-done | bytes 32800 | tf_op jit(solution)/shard_map/while/body/eval_jaxpr/ppermute | solution.py:12
  172.8 2.4 %collective-permute-done.2 = f32[128,128]{1,0:T(8,128)S(1)} collective-permute-done((f32[128,128]{1,0:T(8,128)S(1)}, f32[128,128]{1,0:T(8,128)S(1)}, u32[]{:S(2)}, u32[]{:S(2)}) %collective-permute-start.2) | collective-permute-done | bytes 65568 | tf_op jit(solution)/shard_map/while/body/eval_jaxpr/ppermute | solution.py:12
  175.2 0.7 collective-permute-done.3
  176.0 0.6 dynamic_slice.79
  178.9 3.1 %collective-permute-done = bf16[128,128]{1,0:T(8,128)(2,1)S(1)} collective-permute-done((bf16[128,128]{1,0:T(8,128)(2,1)S(1)}, bf16[128,128]{1,0:T(8,128)(2,1)S(1)}, u32[]{:S(2)}, u32[]{:S(2)}) %collective-permute-start) | collective-permute-done | bytes 32800 | tf_op jit(solution)/shard_map/while/body/eval_jaxpr/ppermute | solution.py:12
  182.3 2.4 %collective-permute-done.2 = f32[128,128]{1,0:T(8,128)S(1)} collective-permute-done((f32[128,128]{1,0:T(8,128)S(1)}, f32[128,128]{1,0:T(8,128)S(1)}, u32[]{:S(2)}, u32[]{:S(2)}) %collective-permute-start.2) | collective-permute-done | bytes 65568 | tf_op jit(solution)/shard_map/while/body/eval_jaxpr/ppermute | solution.py:12
  184.7 0.7 collective-permute-done.3
  188.4 3.1 %collective-permute-done = bf16[128,128]{1,0:T(8,128)(2,1)S(1)} collective-permute-done((bf16[128,128]{1,0:T(8,128)(2,1)S(1)}, bf16[128,128]{1,0:T(8,128)(2,1)S(1)}, u32[]{:S(2)}, u32[]{:S(2)}) %collective-permute-start) | collective-permute-done | bytes 32800 | tf_op jit(solution)/shard_map/while/body/eval_jaxpr/ppermute | solution.py:12
  191.8 2.4 %collective-permute-done.2 = f32[128,128]{1,0:T(8,128)S(1)} collective-permute-done((f32[128,128]{1,0:T(8,128)S(1)}, f32[128,128]{1,0:T(8,128)S(1)}, u32[]{:S(2)}, u32[]{:S(2)}) %collective-permute-start.2) | collective-permute-done | bytes 65568 | tf_op jit(solution)/shard_map/while/body/eval_jaxpr/ppermute | solution.py:12
  194.3 0.7 collective-permute-done.3
  197.9 3.1 %collective-permute-done = bf16[128,128]{1,0:T(8,128)(2,1)S(1)} collective-permute-done((bf16[128,128]{1,0:T(8,128)(2,1)S(1)}, bf16[128,128]{1,0:T(8,128)(2,1)S(1)}, u32[]{:S(2)}, u32[]{:S(2)}) %collective-permute-start) | collective-permute-done | bytes 32800 | tf_op jit(solution)/shard_map/while/body/eval_jaxpr/ppermute | solution.py:12
  201.4 2.4 %collective-permute-done.2 = f32[128,128]{1,0:T(8,128)S(1)} collective-permute-done((f32[128,128]{1,0:T(8,128)S(1)}, f32[128,128]{1,0:T(8,128)S(1)}, u32[]{:S(2)}, u32[]{:S(2)}) %collective-permute-start.2) | collective-permute-done | bytes 65568 | tf_op jit(solution)/shard_map/while/body/eval_jaxpr/ppermute | solution.py:12
  203.8 0.7 collective-permute-done.3
  207.5 3.1 %collective-permute-done = bf16[128,128]{1,0:T(8,128)(2,1)S(1)} collective-permute-done((bf16[128,128]{1,0:T(8,128)(2,1)S(1)}, bf16[128,128]{1,0:T(8,128)(2,1)S(1)}, u32[]{:S(2)}, u32[]{:S(2)}) %collective-permute-start) | collective-permute-done | bytes 32800 | tf_op jit(solution)/shard_map/while/body/eval_jaxpr/ppermute | solution.py:12
  210.9 2.4 %collective-permute-done.2 = f32[128,128]{1,0:T(8,128)S(1)} collective-permute-done((f32[128,128]{1,0:T(8,128)S(1)}, f32[128,128]{1,0:T(8,128)S(1)}, u32[]{:S(2)}, u32[]{:S(2)}) %collective-permute-start.2) | collective-permute-done | bytes 65568 | tf_op jit(solution)/shard_map/while/body/eval_jaxpr/ppermute | solution.py:12
  213.3 0.7 collective-permute-done.3
  215.2 0.7 copy.41
  216.0 0.7 copy.40
  216.7 4.2 %collective-permute-done.5 = f32[128,128]{1,0:T(8,128)S(1)} collective-permute-done((f32[128,128]{1,0:T(8,128)S(1)}, f32[128,128]{1,0:T(8,128)S(1)}, u32[]{:S(2)}, u32[]{:S(2)}) %collective-permute-start.5) | collective-permute-done | bytes 65568 | tf_op jit(solution)/shard_map/ppermute | solution.py:12
  220.9 0.7 collective-permute-done.4
  221.7 0.6 copy.85
  222.3 0.6 copy.86
  (489 shorter events, 55.5 us)
Async XLA Ops:
  0.6 6.1 %copy-start = (bf16[128,512]{1,0:T(8,128)(2,1)S(1)}, bf16[128,512]{1,0:T(8,128)(2,1)}, u32[]{:S(2)}) copy-start(bf16[128,512]{1,0:T(8,128)(2,1)} %param.10) | copy-start | bytes 393220
  50.2 17.7 %copy-start.1 = (bf16[128,512]{1,0:T(8,128)(2,1)S(1)}, bf16[128,512]{1,0:T(8,128)(2,1)}, u32[]{:S(2)}) copy-start(bf16[128,512]{1,0:T(8,128)(2,1)} %param.13) | copy-start | bytes 393220
  69.3 6.1 %collective-permute-start = (bf16[128,128]{1,0:T(8,128)(2,1)S(1)}, bf16[128,128]{1,0:T(8,128)(2,1)S(1)}, u32[]{:S(2)}, u32[]{:S(2)}) collective-permute-start(bf16[128,128]{1,0:T(8,128)(2,1)S(1)} %copy.67), channel_id=1, source_target_pairs={{0,1},{1,2},{2,3},{3,4},{4,5},{5,6},{6,7},{7,8},{8,9},{9,10},{10,1... | collective-permute-start | bytes 98312 | tf_op jit(solution)/shard_map/while/body/eval_jaxpr/ppermute | solution.py:12
  69.7 6.0 %collective-permute-start.1 = (bf16[128,128]{1,0:T(8,128)(2,1)S(1)}, bf16[128,128]{1,0:T(8,128)(2,1)S(1)}, u32[]{:S(2)}, u32[]{:S(2)}) collective-permute-start(bf16[128,128]{1,0:T(8,128)(2,1)S(1)} %copy.68), channel_id=1, source_target_pairs={{0,1},{1,2},{2,3},{3,4},{4,5},{5,6},{6,7},{7,8},{8,9},{9,10},{10,1... | collective-permute-start | bytes 98312 | tf_op jit(solution)/shard_map/while/body/eval_jaxpr/ppermute | solution.py:12
  73.4 6.4 %collective-permute-start.2 = (f32[128,128]{1,0:T(8,128)S(1)}, f32[128,128]{1,0:T(8,128)S(1)}, u32[]{:S(2)}, u32[]{:S(2)}) collective-permute-start(f32[128,128]{1,0:T(8,128)S(1)} %fusion.122), channel_id=1, source_target_pairs={{0,1},{1,2},{2,3},{3,4},{4,5},{5,6},{6,7},{7,8},{8,9},{9,10},{10,1... | collective-permute-start | bytes 196616 | tf_op jit(solution)/shard_map/while/body/eval_jaxpr/ppermute | solution.py:12
  74.1 6.5 %collective-permute-start.3 = (f32[128,128]{1,0:T(8,128)S(1)}, f32[128,128]{1,0:T(8,128)S(1)}, u32[]{:S(2)}, u32[]{:S(2)}) collective-permute-start(f32[128,128]{1,0:T(8,128)S(1)} %convolution_add_fusion.6), channel_id=1, source_target_pairs={{0,1},{1,2},{2,3},{3,4},{4,5},{5,6},{6,7},{7,8},{8,9},{9,10},{10,1... | collective-permute-start | bytes 196616 | tf_op jit(solution)/shard_map/while/body/eval_jaxpr/ppermute | solution.py:12
  80.6 6.0 %collective-permute-start = (bf16[128,128]{1,0:T(8,128)(2,1)S(1)}, bf16[128,128]{1,0:T(8,128)(2,1)S(1)}, u32[]{:S(2)}, u32[]{:S(2)}) collective-permute-start(bf16[128,128]{1,0:T(8,128)(2,1)S(1)} %copy.67), channel_id=1, source_target_pairs={{0,1},{1,2},{2,3},{3,4},{4,5},{5,6},{6,7},{7,8},{8,9},{9,10},{10,1... | collective-permute-start | bytes 98312 | tf_op jit(solution)/shard_map/while/body/eval_jaxpr/ppermute | solution.py:12
  80.6 6.4 %collective-permute-start.1 = (bf16[128,128]{1,0:T(8,128)(2,1)S(1)}, bf16[128,128]{1,0:T(8,128)(2,1)S(1)}, u32[]{:S(2)}, u32[]{:S(2)}) collective-permute-start(bf16[128,128]{1,0:T(8,128)(2,1)S(1)} %copy.68), channel_id=1, source_target_pairs={{0,1},{1,2},{2,3},{3,4},{4,5},{5,6},{6,7},{7,8},{8,9},{9,10},{10,1... | collective-permute-start | bytes 98312 | tf_op jit(solution)/shard_map/while/body/eval_jaxpr/ppermute | solution.py:12
  83.0 6.4 %collective-permute-start.2 = (f32[128,128]{1,0:T(8,128)S(1)}, f32[128,128]{1,0:T(8,128)S(1)}, u32[]{:S(2)}, u32[]{:S(2)}) collective-permute-start(f32[128,128]{1,0:T(8,128)S(1)} %fusion.122), channel_id=1, source_target_pairs={{0,1},{1,2},{2,3},{3,4},{4,5},{5,6},{6,7},{7,8},{8,9},{9,10},{10,1... | collective-permute-start | bytes 196616 | tf_op jit(solution)/shard_map/while/body/eval_jaxpr/ppermute | solution.py:12
  83.3 6.8 %collective-permute-start.3 = (f32[128,128]{1,0:T(8,128)S(1)}, f32[128,128]{1,0:T(8,128)S(1)}, u32[]{:S(2)}, u32[]{:S(2)}) collective-permute-start(f32[128,128]{1,0:T(8,128)S(1)} %convolution_add_fusion.6), channel_id=1, source_target_pairs={{0,1},{1,2},{2,3},{3,4},{4,5},{5,6},{6,7},{7,8},{8,9},{9,10},{10,1... | collective-permute-start | bytes 196616 | tf_op jit(solution)/shard_map/while/body/eval_jaxpr/ppermute | solution.py:12
  90.1 6.0 %collective-permute-start = (bf16[128,128]{1,0:T(8,128)(2,1)S(1)}, bf16[128,128]{1,0:T(8,128)(2,1)S(1)}, u32[]{:S(2)}, u32[]{:S(2)}) collective-permute-start(bf16[128,128]{1,0:T(8,128)(2,1)S(1)} %copy.67), channel_id=1, source_target_pairs={{0,1},{1,2},{2,3},{3,4},{4,5},{5,6},{6,7},{7,8},{8,9},{9,10},{10,1... | collective-permute-start | bytes 98312 | tf_op jit(solution)/shard_map/while/body/eval_jaxpr/ppermute | solution.py:12
  90.1 6.4 %collective-permute-start.1 = (bf16[128,128]{1,0:T(8,128)(2,1)S(1)}, bf16[128,128]{1,0:T(8,128)(2,1)S(1)}, u32[]{:S(2)}, u32[]{:S(2)}) collective-permute-start(bf16[128,128]{1,0:T(8,128)(2,1)S(1)} %copy.68), channel_id=1, source_target_pairs={{0,1},{1,2},{2,3},{3,4},{4,5},{5,6},{6,7},{7,8},{8,9},{9,10},{10,1... | collective-permute-start | bytes 98312 | tf_op jit(solution)/shard_map/while/body/eval_jaxpr/ppermute | solution.py:12
  92.5 6.4 %collective-permute-start.2 = (f32[128,128]{1,0:T(8,128)S(1)}, f32[128,128]{1,0:T(8,128)S(1)}, u32[]{:S(2)}, u32[]{:S(2)}) collective-permute-start(f32[128,128]{1,0:T(8,128)S(1)} %fusion.122), channel_id=1, source_target_pairs={{0,1},{1,2},{2,3},{3,4},{4,5},{5,6},{6,7},{7,8},{8,9},{9,10},{10,1... | collective-permute-start | bytes 196616 | tf_op jit(solution)/shard_map/while/body/eval_jaxpr/ppermute | solution.py:12
  92.8 6.8 %collective-permute-start.3 = (f32[128,128]{1,0:T(8,128)S(1)}, f32[128,128]{1,0:T(8,128)S(1)}, u32[]{:S(2)}, u32[]{:S(2)}) collective-permute-start(f32[128,128]{1,0:T(8,128)S(1)} %convolution_add_fusion.6), channel_id=1, source_target_pairs={{0,1},{1,2},{2,3},{3,4},{4,5},{5,6},{6,7},{7,8},{8,9},{9,10},{10,1... | collective-permute-start | bytes 196616 | tf_op jit(solution)/shard_map/while/body/eval_jaxpr/ppermute | solution.py:12
  99.6 6.0 %collective-permute-start = (bf16[128,128]{1,0:T(8,128)(2,1)S(1)}, bf16[128,128]{1,0:T(8,128)(2,1)S(1)}, u32[]{:S(2)}, u32[]{:S(2)}) collective-permute-start(bf16[128,128]{1,0:T(8,128)(2,1)S(1)} %copy.67), channel_id=1, source_target_pairs={{0,1},{1,2},{2,3},{3,4},{4,5},{5,6},{6,7},{7,8},{8,9},{9,10},{10,1... | collective-permute-start | bytes 98312 | tf_op jit(solution)/shard_map/while/body/eval_jaxpr/ppermute | solution.py:12
  99.7 6.4 %collective-permute-start.1 = (bf16[128,128]{1,0:T(8,128)(2,1)S(1)}, bf16[128,128]{1,0:T(8,128)(2,1)S(1)}, u32[]{:S(2)}, u32[]{:S(2)}) collective-permute-start(bf16[128,128]{1,0:T(8,128)(2,1)S(1)} %copy.68), channel_id=1, source_target_pairs={{0,1},{1,2},{2,3},{3,4},{4,5},{5,6},{6,7},{7,8},{8,9},{9,10},{10,1... | collective-permute-start | bytes 98312 | tf_op jit(solution)/shard_map/while/body/eval_jaxpr/ppermute | solution.py:12
  102.0 6.4 %collective-permute-start.2 = (f32[128,128]{1,0:T(8,128)S(1)}, f32[128,128]{1,0:T(8,128)S(1)}, u32[]{:S(2)}, u32[]{:S(2)}) collective-permute-start(f32[128,128]{1,0:T(8,128)S(1)} %fusion.122), channel_id=1, source_target_pairs={{0,1},{1,2},{2,3},{3,4},{4,5},{5,6},{6,7},{7,8},{8,9},{9,10},{10,1... | collective-permute-start | bytes 196616 | tf_op jit(solution)/shard_map/while/body/eval_jaxpr/ppermute | solution.py:12
  102.3 6.8 %collective-permute-start.3 = (f32[128,128]{1,0:T(8,128)S(1)}, f32[128,128]{1,0:T(8,128)S(1)}, u32[]{:S(2)}, u32[]{:S(2)}) collective-permute-start(f32[128,128]{1,0:T(8,128)S(1)} %convolution_add_fusion.6), channel_id=1, source_target_pairs={{0,1},{1,2},{2,3},{3,4},{4,5},{5,6},{6,7},{7,8},{8,9},{9,10},{10,1... | collective-permute-start | bytes 196616 | tf_op jit(solution)/shard_map/while/body/eval_jaxpr/ppermute | solution.py:12
  109.2 6.0 %collective-permute-start = (bf16[128,128]{1,0:T(8,128)(2,1)S(1)}, bf16[128,128]{1,0:T(8,128)(2,1)S(1)}, u32[]{:S(2)}, u32[]{:S(2)}) collective-permute-start(bf16[128,128]{1,0:T(8,128)(2,1)S(1)} %copy.67), channel_id=1, source_target_pairs={{0,1},{1,2},{2,3},{3,4},{4,5},{5,6},{6,7},{7,8},{8,9},{9,10},{10,1... | collective-permute-start | bytes 98312 | tf_op jit(solution)/shard_map/while/body/eval_jaxpr/ppermute | solution.py:12
  109.2 6.4 %collective-permute-start.1 = (bf16[128,128]{1,0:T(8,128)(2,1)S(1)}, bf16[128,128]{1,0:T(8,128)(2,1)S(1)}, u32[]{:S(2)}, u32[]{:S(2)}) collective-permute-start(bf16[128,128]{1,0:T(8,128)(2,1)S(1)} %copy.68), channel_id=1, source_target_pairs={{0,1},{1,2},{2,3},{3,4},{4,5},{5,6},{6,7},{7,8},{8,9},{9,10},{10,1... | collective-permute-start | bytes 98312 | tf_op jit(solution)/shard_map/while/body/eval_jaxpr/ppermute | solution.py:12
  111.6 6.4 %collective-permute-start.2 = (f32[128,128]{1,0:T(8,128)S(1)}, f32[128,128]{1,0:T(8,128)S(1)}, u32[]{:S(2)}, u32[]{:S(2)}) collective-permute-start(f32[128,128]{1,0:T(8,128)S(1)} %fusion.122), channel_id=1, source_target_pairs={{0,1},{1,2},{2,3},{3,4},{4,5},{5,6},{6,7},{7,8},{8,9},{9,10},{10,1... | collective-permute-start | bytes 196616 | tf_op jit(solution)/shard_map/while/body/eval_jaxpr/ppermute | solution.py:12
  111.9 6.8 %collective-permute-start.3 = (f32[128,128]{1,0:T(8,128)S(1)}, f32[128,128]{1,0:T(8,128)S(1)}, u32[]{:S(2)}, u32[]{:S(2)}) collective-permute-start(f32[128,128]{1,0:T(8,128)S(1)} %convolution_add_fusion.6), channel_id=1, source_target_pairs={{0,1},{1,2},{2,3},{3,4},{4,5},{5,6},{6,7},{7,8},{8,9},{9,10},{10,1... | collective-permute-start | bytes 196616 | tf_op jit(solution)/shard_map/while/body/eval_jaxpr/ppermute | solution.py:12
  118.7 6.0 %collective-permute-start = (bf16[128,128]{1,0:T(8,128)(2,1)S(1)}, bf16[128,128]{1,0:T(8,128)(2,1)S(1)}, u32[]{:S(2)}, u32[]{:S(2)}) collective-permute-start(bf16[128,128]{1,0:T(8,128)(2,1)S(1)} %copy.67), channel_id=1, source_target_pairs={{0,1},{1,2},{2,3},{3,4},{4,5},{5,6},{6,7},{7,8},{8,9},{9,10},{10,1... | collective-permute-start | bytes 98312 | tf_op jit(solution)/shard_map/while/body/eval_jaxpr/ppermute | solution.py:12
  118.7 6.4 %collective-permute-start.1 = (bf16[128,128]{1,0:T(8,128)(2,1)S(1)}, bf16[128,128]{1,0:T(8,128)(2,1)S(1)}, u32[]{:S(2)}, u32[]{:S(2)}) collective-permute-start(bf16[128,128]{1,0:T(8,128)(2,1)S(1)} %copy.68), channel_id=1, source_target_pairs={{0,1},{1,2},{2,3},{3,4},{4,5},{5,6},{6,7},{7,8},{8,9},{9,10},{10,1... | collective-permute-start | bytes 98312 | tf_op jit(solution)/shard_map/while/body/eval_jaxpr/ppermute | solution.py:12
  121.1 6.4 %collective-permute-start.2 = (f32[128,128]{1,0:T(8,128)S(1)}, f32[128,128]{1,0:T(8,128)S(1)}, u32[]{:S(2)}, u32[]{:S(2)}) collective-permute-start(f32[128,128]{1,0:T(8,128)S(1)} %fusion.122), channel_id=1, source_target_pairs={{0,1},{1,2},{2,3},{3,4},{4,5},{5,6},{6,7},{7,8},{8,9},{9,10},{10,1... | collective-permute-start | bytes 196616 | tf_op jit(solution)/shard_map/while/body/eval_jaxpr/ppermute | solution.py:12
  121.4 6.8 %collective-permute-start.3 = (f32[128,128]{1,0:T(8,128)S(1)}, f32[128,128]{1,0:T(8,128)S(1)}, u32[]{:S(2)}, u32[]{:S(2)}) collective-permute-start(f32[128,128]{1,0:T(8,128)S(1)} %convolution_add_fusion.6), channel_id=1, source_target_pairs={{0,1},{1,2},{2,3},{3,4},{4,5},{5,6},{6,7},{7,8},{8,9},{9,10},{10,1... | collective-permute-start | bytes 196616 | tf_op jit(solution)/shard_map/while/body/eval_jaxpr/ppermute | solution.py:12
  128.2 6.0 %collective-permute-start = (bf16[128,128]{1,0:T(8,128)(2,1)S(1)}, bf16[128,128]{1,0:T(8,128)(2,1)S(1)}, u32[]{:S(2)}, u32[]{:S(2)}) collective-permute-start(bf16[128,128]{1,0:T(8,128)(2,1)S(1)} %copy.67), channel_id=1, source_target_pairs={{0,1},{1,2},{2,3},{3,4},{4,5},{5,6},{6,7},{7,8},{8,9},{9,10},{10,1... | collective-permute-start | bytes 98312 | tf_op jit(solution)/shard_map/while/body/eval_jaxpr/ppermute | solution.py:12
  128.3 6.4 %collective-permute-start.1 = (bf16[128,128]{1,0:T(8,128)(2,1)S(1)}, bf16[128,128]{1,0:T(8,128)(2,1)S(1)}, u32[]{:S(2)}, u32[]{:S(2)}) collective-permute-start(bf16[128,128]{1,0:T(8,128)(2,1)S(1)} %copy.68), channel_id=1, source_target_pairs={{0,1},{1,2},{2,3},{3,4},{4,5},{5,6},{6,7},{7,8},{8,9},{9,10},{10,1... | collective-permute-start | bytes 98312 | tf_op jit(solution)/shard_map/while/body/eval_jaxpr/ppermute | solution.py:12
  130.6 6.4 %collective-permute-start.2 = (f32[128,128]{1,0:T(8,128)S(1)}, f32[128,128]{1,0:T(8,128)S(1)}, u32[]{:S(2)}, u32[]{:S(2)}) collective-permute-start(f32[128,128]{1,0:T(8,128)S(1)} %fusion.122), channel_id=1, source_target_pairs={{0,1},{1,2},{2,3},{3,4},{4,5},{5,6},{6,7},{7,8},{8,9},{9,10},{10,1... | collective-permute-start | bytes 196616 | tf_op jit(solution)/shard_map/while/body/eval_jaxpr/ppermute | solution.py:12
  130.9 6.8 %collective-permute-start.3 = (f32[128,128]{1,0:T(8,128)S(1)}, f32[128,128]{1,0:T(8,128)S(1)}, u32[]{:S(2)}, u32[]{:S(2)}) collective-permute-start(f32[128,128]{1,0:T(8,128)S(1)} %convolution_add_fusion.6), channel_id=1, source_target_pairs={{0,1},{1,2},{2,3},{3,4},{4,5},{5,6},{6,7},{7,8},{8,9},{9,10},{10,1... | collective-permute-start | bytes 196616 | tf_op jit(solution)/shard_map/while/body/eval_jaxpr/ppermute | solution.py:12
  137.8 6.0 %collective-permute-start = (bf16[128,128]{1,0:T(8,128)(2,1)S(1)}, bf16[128,128]{1,0:T(8,128)(2,1)S(1)}, u32[]{:S(2)}, u32[]{:S(2)}) collective-permute-start(bf16[128,128]{1,0:T(8,128)(2,1)S(1)} %copy.67), channel_id=1, source_target_pairs={{0,1},{1,2},{2,3},{3,4},{4,5},{5,6},{6,7},{7,8},{8,9},{9,10},{10,1... | collective-permute-start | bytes 98312 | tf_op jit(solution)/shard_map/while/body/eval_jaxpr/ppermute | solution.py:12
  137.8 6.4 %collective-permute-start.1 = (bf16[128,128]{1,0:T(8,128)(2,1)S(1)}, bf16[128,128]{1,0:T(8,128)(2,1)S(1)}, u32[]{:S(2)}, u32[]{:S(2)}) collective-permute-start(bf16[128,128]{1,0:T(8,128)(2,1)S(1)} %copy.68), channel_id=1, source_target_pairs={{0,1},{1,2},{2,3},{3,4},{4,5},{5,6},{6,7},{7,8},{8,9},{9,10},{10,1... | collective-permute-start | bytes 98312 | tf_op jit(solution)/shard_map/while/body/eval_jaxpr/ppermute | solution.py:12
  140.2 6.4 %collective-permute-start.2 = (f32[128,128]{1,0:T(8,128)S(1)}, f32[128,128]{1,0:T(8,128)S(1)}, u32[]{:S(2)}, u32[]{:S(2)}) collective-permute-start(f32[128,128]{1,0:T(8,128)S(1)} %fusion.122), channel_id=1, source_target_pairs={{0,1},{1,2},{2,3},{3,4},{4,5},{5,6},{6,7},{7,8},{8,9},{9,10},{10,1... | collective-permute-start | bytes 196616 | tf_op jit(solution)/shard_map/while/body/eval_jaxpr/ppermute | solution.py:12
  140.5 6.8 %collective-permute-start.3 = (f32[128,128]{1,0:T(8,128)S(1)}, f32[128,128]{1,0:T(8,128)S(1)}, u32[]{:S(2)}, u32[]{:S(2)}) collective-permute-start(f32[128,128]{1,0:T(8,128)S(1)} %convolution_add_fusion.6), channel_id=1, source_target_pairs={{0,1},{1,2},{2,3},{3,4},{4,5},{5,6},{6,7},{7,8},{8,9},{9,10},{10,1... | collective-permute-start | bytes 196616 | tf_op jit(solution)/shard_map/while/body/eval_jaxpr/ppermute | solution.py:12
  147.3 6.0 %collective-permute-start = (bf16[128,128]{1,0:T(8,128)(2,1)S(1)}, bf16[128,128]{1,0:T(8,128)(2,1)S(1)}, u32[]{:S(2)}, u32[]{:S(2)}) collective-permute-start(bf16[128,128]{1,0:T(8,128)(2,1)S(1)} %copy.67), channel_id=1, source_target_pairs={{0,1},{1,2},{2,3},{3,4},{4,5},{5,6},{6,7},{7,8},{8,9},{9,10},{10,1... | collective-permute-start | bytes 98312 | tf_op jit(solution)/shard_map/while/body/eval_jaxpr/ppermute | solution.py:12
  147.3 6.4 %collective-permute-start.1 = (bf16[128,128]{1,0:T(8,128)(2,1)S(1)}, bf16[128,128]{1,0:T(8,128)(2,1)S(1)}, u32[]{:S(2)}, u32[]{:S(2)}) collective-permute-start(bf16[128,128]{1,0:T(8,128)(2,1)S(1)} %copy.68), channel_id=1, source_target_pairs={{0,1},{1,2},{2,3},{3,4},{4,5},{5,6},{6,7},{7,8},{8,9},{9,10},{10,1... | collective-permute-start | bytes 98312 | tf_op jit(solution)/shard_map/while/body/eval_jaxpr/ppermute | solution.py:12
  149.7 6.4 %collective-permute-start.2 = (f32[128,128]{1,0:T(8,128)S(1)}, f32[128,128]{1,0:T(8,128)S(1)}, u32[]{:S(2)}, u32[]{:S(2)}) collective-permute-start(f32[128,128]{1,0:T(8,128)S(1)} %fusion.122), channel_id=1, source_target_pairs={{0,1},{1,2},{2,3},{3,4},{4,5},{5,6},{6,7},{7,8},{8,9},{9,10},{10,1... | collective-permute-start | bytes 196616 | tf_op jit(solution)/shard_map/while/body/eval_jaxpr/ppermute | solution.py:12
  150.0 6.8 %collective-permute-start.3 = (f32[128,128]{1,0:T(8,128)S(1)}, f32[128,128]{1,0:T(8,128)S(1)}, u32[]{:S(2)}, u32[]{:S(2)}) collective-permute-start(f32[128,128]{1,0:T(8,128)S(1)} %convolution_add_fusion.6), channel_id=1, source_target_pairs={{0,1},{1,2},{2,3},{3,4},{4,5},{5,6},{6,7},{7,8},{8,9},{9,10},{10,1... | collective-permute-start | bytes 196616 | tf_op jit(solution)/shard_map/while/body/eval_jaxpr/ppermute | solution.py:12
  156.8 6.0 %collective-permute-start = (bf16[128,128]{1,0:T(8,128)(2,1)S(1)}, bf16[128,128]{1,0:T(8,128)(2,1)S(1)}, u32[]{:S(2)}, u32[]{:S(2)}) collective-permute-start(bf16[128,128]{1,0:T(8,128)(2,1)S(1)} %copy.67), channel_id=1, source_target_pairs={{0,1},{1,2},{2,3},{3,4},{4,5},{5,6},{6,7},{7,8},{8,9},{9,10},{10,1... | collective-permute-start | bytes 98312 | tf_op jit(solution)/shard_map/while/body/eval_jaxpr/ppermute | solution.py:12
  156.9 6.4 %collective-permute-start.1 = (bf16[128,128]{1,0:T(8,128)(2,1)S(1)}, bf16[128,128]{1,0:T(8,128)(2,1)S(1)}, u32[]{:S(2)}, u32[]{:S(2)}) collective-permute-start(bf16[128,128]{1,0:T(8,128)(2,1)S(1)} %copy.68), channel_id=1, source_target_pairs={{0,1},{1,2},{2,3},{3,4},{4,5},{5,6},{6,7},{7,8},{8,9},{9,10},{10,1... | collective-permute-start | bytes 98312 | tf_op jit(solution)/shard_map/while/body/eval_jaxpr/ppermute | solution.py:12
  159.2 6.4 %collective-permute-start.2 = (f32[128,128]{1,0:T(8,128)S(1)}, f32[128,128]{1,0:T(8,128)S(1)}, u32[]{:S(2)}, u32[]{:S(2)}) collective-permute-start(f32[128,128]{1,0:T(8,128)S(1)} %fusion.122), channel_id=1, source_target_pairs={{0,1},{1,2},{2,3},{3,4},{4,5},{5,6},{6,7},{7,8},{8,9},{9,10},{10,1... | collective-permute-start | bytes 196616 | tf_op jit(solution)/shard_map/while/body/eval_jaxpr/ppermute | solution.py:12
  159.5 6.8 %collective-permute-start.3 = (f32[128,128]{1,0:T(8,128)S(1)}, f32[128,128]{1,0:T(8,128)S(1)}, u32[]{:S(2)}, u32[]{:S(2)}) collective-permute-start(f32[128,128]{1,0:T(8,128)S(1)} %convolution_add_fusion.6), channel_id=1, source_target_pairs={{0,1},{1,2},{2,3},{3,4},{4,5},{5,6},{6,7},{7,8},{8,9},{9,10},{10,1... | collective-permute-start | bytes 196616 | tf_op jit(solution)/shard_map/while/body/eval_jaxpr/ppermute | solution.py:12
  166.4 6.0 %collective-permute-start = (bf16[128,128]{1,0:T(8,128)(2,1)S(1)}, bf16[128,128]{1,0:T(8,128)(2,1)S(1)}, u32[]{:S(2)}, u32[]{:S(2)}) collective-permute-start(bf16[128,128]{1,0:T(8,128)(2,1)S(1)} %copy.67), channel_id=1, source_target_pairs={{0,1},{1,2},{2,3},{3,4},{4,5},{5,6},{6,7},{7,8},{8,9},{9,10},{10,1... | collective-permute-start | bytes 98312 | tf_op jit(solution)/shard_map/while/body/eval_jaxpr/ppermute | solution.py:12
  166.4 6.4 %collective-permute-start.1 = (bf16[128,128]{1,0:T(8,128)(2,1)S(1)}, bf16[128,128]{1,0:T(8,128)(2,1)S(1)}, u32[]{:S(2)}, u32[]{:S(2)}) collective-permute-start(bf16[128,128]{1,0:T(8,128)(2,1)S(1)} %copy.68), channel_id=1, source_target_pairs={{0,1},{1,2},{2,3},{3,4},{4,5},{5,6},{6,7},{7,8},{8,9},{9,10},{10,1... | collective-permute-start | bytes 98312 | tf_op jit(solution)/shard_map/while/body/eval_jaxpr/ppermute | solution.py:12
  168.8 6.4 %collective-permute-start.2 = (f32[128,128]{1,0:T(8,128)S(1)}, f32[128,128]{1,0:T(8,128)S(1)}, u32[]{:S(2)}, u32[]{:S(2)}) collective-permute-start(f32[128,128]{1,0:T(8,128)S(1)} %fusion.122), channel_id=1, source_target_pairs={{0,1},{1,2},{2,3},{3,4},{4,5},{5,6},{6,7},{7,8},{8,9},{9,10},{10,1... | collective-permute-start | bytes 196616 | tf_op jit(solution)/shard_map/while/body/eval_jaxpr/ppermute | solution.py:12
  169.1 6.8 %collective-permute-start.3 = (f32[128,128]{1,0:T(8,128)S(1)}, f32[128,128]{1,0:T(8,128)S(1)}, u32[]{:S(2)}, u32[]{:S(2)}) collective-permute-start(f32[128,128]{1,0:T(8,128)S(1)} %convolution_add_fusion.6), channel_id=1, source_target_pairs={{0,1},{1,2},{2,3},{3,4},{4,5},{5,6},{6,7},{7,8},{8,9},{9,10},{10,1... | collective-permute-start | bytes 196616 | tf_op jit(solution)/shard_map/while/body/eval_jaxpr/ppermute | solution.py:12
  175.9 6.0 %collective-permute-start = (bf16[128,128]{1,0:T(8,128)(2,1)S(1)}, bf16[128,128]{1,0:T(8,128)(2,1)S(1)}, u32[]{:S(2)}, u32[]{:S(2)}) collective-permute-start(bf16[128,128]{1,0:T(8,128)(2,1)S(1)} %copy.67), channel_id=1, source_target_pairs={{0,1},{1,2},{2,3},{3,4},{4,5},{5,6},{6,7},{7,8},{8,9},{9,10},{10,1... | collective-permute-start | bytes 98312 | tf_op jit(solution)/shard_map/while/body/eval_jaxpr/ppermute | solution.py:12
  175.9 6.4 %collective-permute-start.1 = (bf16[128,128]{1,0:T(8,128)(2,1)S(1)}, bf16[128,128]{1,0:T(8,128)(2,1)S(1)}, u32[]{:S(2)}, u32[]{:S(2)}) collective-permute-start(bf16[128,128]{1,0:T(8,128)(2,1)S(1)} %copy.68), channel_id=1, source_target_pairs={{0,1},{1,2},{2,3},{3,4},{4,5},{5,6},{6,7},{7,8},{8,9},{9,10},{10,1... | collective-permute-start | bytes 98312 | tf_op jit(solution)/shard_map/while/body/eval_jaxpr/ppermute | solution.py:12
  178.3 6.4 %collective-permute-start.2 = (f32[128,128]{1,0:T(8,128)S(1)}, f32[128,128]{1,0:T(8,128)S(1)}, u32[]{:S(2)}, u32[]{:S(2)}) collective-permute-start(f32[128,128]{1,0:T(8,128)S(1)} %fusion.122), channel_id=1, source_target_pairs={{0,1},{1,2},{2,3},{3,4},{4,5},{5,6},{6,7},{7,8},{8,9},{9,10},{10,1... | collective-permute-start | bytes 196616 | tf_op jit(solution)/shard_map/while/body/eval_jaxpr/ppermute | solution.py:12
  178.6 6.8 %collective-permute-start.3 = (f32[128,128]{1,0:T(8,128)S(1)}, f32[128,128]{1,0:T(8,128)S(1)}, u32[]{:S(2)}, u32[]{:S(2)}) collective-permute-start(f32[128,128]{1,0:T(8,128)S(1)} %convolution_add_fusion.6), channel_id=1, source_target_pairs={{0,1},{1,2},{2,3},{3,4},{4,5},{5,6},{6,7},{7,8},{8,9},{9,10},{10,1... | collective-permute-start | bytes 196616 | tf_op jit(solution)/shard_map/while/body/eval_jaxpr/ppermute | solution.py:12
  185.4 6.0 %collective-permute-start = (bf16[128,128]{1,0:T(8,128)(2,1)S(1)}, bf16[128,128]{1,0:T(8,128)(2,1)S(1)}, u32[]{:S(2)}, u32[]{:S(2)}) collective-permute-start(bf16[128,128]{1,0:T(8,128)(2,1)S(1)} %copy.67), channel_id=1, source_target_pairs={{0,1},{1,2},{2,3},{3,4},{4,5},{5,6},{6,7},{7,8},{8,9},{9,10},{10,1... | collective-permute-start | bytes 98312 | tf_op jit(solution)/shard_map/while/body/eval_jaxpr/ppermute | solution.py:12
  185.5 6.4 %collective-permute-start.1 = (bf16[128,128]{1,0:T(8,128)(2,1)S(1)}, bf16[128,128]{1,0:T(8,128)(2,1)S(1)}, u32[]{:S(2)}, u32[]{:S(2)}) collective-permute-start(bf16[128,128]{1,0:T(8,128)(2,1)S(1)} %copy.68), channel_id=1, source_target_pairs={{0,1},{1,2},{2,3},{3,4},{4,5},{5,6},{6,7},{7,8},{8,9},{9,10},{10,1... | collective-permute-start | bytes 98312 | tf_op jit(solution)/shard_map/while/body/eval_jaxpr/ppermute | solution.py:12
  187.8 6.4 %collective-permute-start.2 = (f32[128,128]{1,0:T(8,128)S(1)}, f32[128,128]{1,0:T(8,128)S(1)}, u32[]{:S(2)}, u32[]{:S(2)}) collective-permute-start(f32[128,128]{1,0:T(8,128)S(1)} %fusion.122), channel_id=1, source_target_pairs={{0,1},{1,2},{2,3},{3,4},{4,5},{5,6},{6,7},{7,8},{8,9},{9,10},{10,1... | collective-permute-start | bytes 196616 | tf_op jit(solution)/shard_map/while/body/eval_jaxpr/ppermute | solution.py:12
  188.1 6.8 %collective-permute-start.3 = (f32[128,128]{1,0:T(8,128)S(1)}, f32[128,128]{1,0:T(8,128)S(1)}, u32[]{:S(2)}, u32[]{:S(2)}) collective-permute-start(f32[128,128]{1,0:T(8,128)S(1)} %convolution_add_fusion.6), channel_id=1, source_target_pairs={{0,1},{1,2},{2,3},{3,4},{4,5},{5,6},{6,7},{7,8},{8,9},{9,10},{10,1... | collective-permute-start | bytes 196616 | tf_op jit(solution)/shard_map/while/body/eval_jaxpr/ppermute | solution.py:12
  195.0 6.0 %collective-permute-start = (bf16[128,128]{1,0:T(8,128)(2,1)S(1)}, bf16[128,128]{1,0:T(8,128)(2,1)S(1)}, u32[]{:S(2)}, u32[]{:S(2)}) collective-permute-start(bf16[128,128]{1,0:T(8,128)(2,1)S(1)} %copy.67), channel_id=1, source_target_pairs={{0,1},{1,2},{2,3},{3,4},{4,5},{5,6},{6,7},{7,8},{8,9},{9,10},{10,1... | collective-permute-start | bytes 98312 | tf_op jit(solution)/shard_map/while/body/eval_jaxpr/ppermute | solution.py:12
  195.0 6.4 %collective-permute-start.1 = (bf16[128,128]{1,0:T(8,128)(2,1)S(1)}, bf16[128,128]{1,0:T(8,128)(2,1)S(1)}, u32[]{:S(2)}, u32[]{:S(2)}) collective-permute-start(bf16[128,128]{1,0:T(8,128)(2,1)S(1)} %copy.68), channel_id=1, source_target_pairs={{0,1},{1,2},{2,3},{3,4},{4,5},{5,6},{6,7},{7,8},{8,9},{9,10},{10,1... | collective-permute-start | bytes 98312 | tf_op jit(solution)/shard_map/while/body/eval_jaxpr/ppermute | solution.py:12
  197.4 6.4 %collective-permute-start.2 = (f32[128,128]{1,0:T(8,128)S(1)}, f32[128,128]{1,0:T(8,128)S(1)}, u32[]{:S(2)}, u32[]{:S(2)}) collective-permute-start(f32[128,128]{1,0:T(8,128)S(1)} %fusion.122), channel_id=1, source_target_pairs={{0,1},{1,2},{2,3},{3,4},{4,5},{5,6},{6,7},{7,8},{8,9},{9,10},{10,1... | collective-permute-start | bytes 196616 | tf_op jit(solution)/shard_map/while/body/eval_jaxpr/ppermute | solution.py:12
  197.7 6.8 %collective-permute-start.3 = (f32[128,128]{1,0:T(8,128)S(1)}, f32[128,128]{1,0:T(8,128)S(1)}, u32[]{:S(2)}, u32[]{:S(2)}) collective-permute-start(f32[128,128]{1,0:T(8,128)S(1)} %convolution_add_fusion.6), channel_id=1, source_target_pairs={{0,1},{1,2},{2,3},{3,4},{4,5},{5,6},{6,7},{7,8},{8,9},{9,10},{10,1... | collective-permute-start | bytes 196616 | tf_op jit(solution)/shard_map/while/body/eval_jaxpr/ppermute | solution.py:12
  204.5 6.0 %collective-permute-start = (bf16[128,128]{1,0:T(8,128)(2,1)S(1)}, bf16[128,128]{1,0:T(8,128)(2,1)S(1)}, u32[]{:S(2)}, u32[]{:S(2)}) collective-permute-start(bf16[128,128]{1,0:T(8,128)(2,1)S(1)} %copy.67), channel_id=1, source_target_pairs={{0,1},{1,2},{2,3},{3,4},{4,5},{5,6},{6,7},{7,8},{8,9},{9,10},{10,1... | collective-permute-start | bytes 98312 | tf_op jit(solution)/shard_map/while/body/eval_jaxpr/ppermute | solution.py:12
  204.5 6.4 %collective-permute-start.1 = (bf16[128,128]{1,0:T(8,128)(2,1)S(1)}, bf16[128,128]{1,0:T(8,128)(2,1)S(1)}, u32[]{:S(2)}, u32[]{:S(2)}) collective-permute-start(bf16[128,128]{1,0:T(8,128)(2,1)S(1)} %copy.68), channel_id=1, source_target_pairs={{0,1},{1,2},{2,3},{3,4},{4,5},{5,6},{6,7},{7,8},{8,9},{9,10},{10,1... | collective-permute-start | bytes 98312 | tf_op jit(solution)/shard_map/while/body/eval_jaxpr/ppermute | solution.py:12
  206.9 6.4 %collective-permute-start.2 = (f32[128,128]{1,0:T(8,128)S(1)}, f32[128,128]{1,0:T(8,128)S(1)}, u32[]{:S(2)}, u32[]{:S(2)}) collective-permute-start(f32[128,128]{1,0:T(8,128)S(1)} %fusion.122), channel_id=1, source_target_pairs={{0,1},{1,2},{2,3},{3,4},{4,5},{5,6},{6,7},{7,8},{8,9},{9,10},{10,1... | collective-permute-start | bytes 196616 | tf_op jit(solution)/shard_map/while/body/eval_jaxpr/ppermute | solution.py:12
  207.2 6.8 %collective-permute-start.3 = (f32[128,128]{1,0:T(8,128)S(1)}, f32[128,128]{1,0:T(8,128)S(1)}, u32[]{:S(2)}, u32[]{:S(2)}) collective-permute-start(f32[128,128]{1,0:T(8,128)S(1)} %convolution_add_fusion.6), channel_id=1, source_target_pairs={{0,1},{1,2},{2,3},{3,4},{4,5},{5,6},{6,7},{7,8},{8,9},{9,10},{10,1... | collective-permute-start | bytes 196616 | tf_op jit(solution)/shard_map/while/body/eval_jaxpr/ppermute | solution.py:12
  214.5 6.4 %collective-permute-start.5 = (f32[128,128]{1,0:T(8,128)S(1)}, f32[128,128]{1,0:T(8,128)S(1)}, u32[]{:S(2)}, u32[]{:S(2)}) collective-permute-start(f32[128,128]{1,0:T(8,128)S(1)} %convolution_add_fusion.2), channel_id=1, source_target_pairs={{0,1},{1,2},{2,3},{3,4},{4,5},{5,6},{6,7},{7,8},{8,9},{9,10},{10,1... | collective-permute-start | bytes 196616 | tf_op jit(solution)/shard_map/ppermute | solution.py:12
  215.0 6.7 %collective-permute-start.4 = (f32[128,128]{1,0:T(8,128)S(1)}, f32[128,128]{1,0:T(8,128)S(1)}, u32[]{:S(2)}, u32[]{:S(2)}) collective-permute-start(f32[128,128]{1,0:T(8,128)S(1)} %fusion.45), channel_id=1, source_target_pairs={{0,1},{1,2},{2,3},{3,4},{4,5},{5,6},{6,7},{7,8},{8,9},{9,10},{10,1... | collective-permute-start | bytes 196616 | tf_op jit(solution)/shard_map/ppermute | solution.py:12
  (2 other events, 1.5 us)
where the time goes:
time: 223 us
  waiting for transfers between devices  103 us (46%)
  blocking collectives  43.4 us (19%)
  matrix products  31.7 us (14%)
  local copies, waits for them, and re-layouts  17 us (8%)
  loops' own time  13 us (6%)
  other arithmetic  5.81 us (3%)
  starting transfers between devices  5 us (2%)
  between operations  4.08 us (2%)
    ppermute x62, waiting for transfers between devices, passed_along(): return lax.ppermute(value, axis, pairs)  103 us
    all_gather x1, blocking collectives, shards(): key_piece = lax.all_gather(key_states, 'blk', axis=0, tiled=True)  24.6 us
    all_gather x1, blocking collectives, shards(): value_piece = lax.all_gather(value_states, 'blk', axis=0, tiled=True)  18.9 us
    another operation x1, loops' own time, shards(): carry_state = lax.fori_loop(0, cycle_size - 1, key_turn, carry_state)  11.7 us
    dynamic_slice x16, local copies, waits for them, and re-layouts, key_step(): key_pos = block_order[source] * tok_rows + offsets  9.38 us
    dot_general x32, matrix products, mask_for(): jnp.dot(tile_rows, one_hot.T, preferred_element_type=jnp.float32) > 0.5  6.53 us
    ppermute x62, starting transfers between devices, passed_along(): return lax.ppermute(value, axis, pairs)  5 us
    dot_general x16, matrix products, softmax_update(): jnp.dot(weights.astype(jnp.bfloat16), value_sub, preferred_element_type=j...  4.83 us
  transfers between devices with their start and end apart: 62, of which 62 were waited for; matrix products, arithmetic and copies ran while one was open for 14% of the time, Pallas kernels for 0%

commit v1 on v0

--- a/solution.py
+++ b/solution.py
@@ -2,6 +2,7 @@
 import jax.numpy as jnp
 from jax import lax
 from jax.sharding import PartitionSpec as P
+from jax.lax import all_gather
 
 TILE = 128
 
@@ -80,8 +81,11 @@
         jnp.zeros((total_rows,), jnp.float32),
         jnp.zeros((total_rows, head_width), jnp.float32),
     )
-    key_piece = lax.all_gather(key_states, "blk", axis=0, tiled=True)
-    value_piece = lax.all_gather(value_states, "blk", axis=0, tiled=True)
+    key_piece, value_piece = jnp.split(
+        all_gather(jnp.concatenate([key_states, value_states], axis=1), "blk", axis=0, tiled=True),
+        [key_states.shape[1]],
+        axis=1,
+    )
     piece_rows = key_piece.shape[0]
 
     def sub_step(sub_num, inner_state):

time: 223 us -> 230 us (1.031)
  blocking collectives: 43.4 us -> 0 us
  waiting for transfers between devices: 103 us -> 136 us
  between operations: 4.08 us -> 17.4 us
    all_gather x2 -> x0, blocking collectives: 43.4 us -> none  [the longest x1 24.6 us: shards(): key_piece = lax.all_gather(key_states, 'blk', axis=0, tiled=True)]
    all_gather x0 -> x1, waiting for transfers between devices: none -> 35.6 us  [shards(): all_gather(jnp.concatenate([key_states, value_states], axis=1), 'blk', ax...]
  transfers between devices with their start and end apart: 62 -> 63, of which waited for: 62 -> 63; matrix products, arithmetic and copies ran while one was open for 14% -> 15% of each run, Pallas kernels for 0% -> 0%
where the time goes in v1:
time: 230 us
  waiting for transfers between devices  136 us (59%)
  matrix products  31.7 us (14%)
  local copies, waits for them, and re-layouts  19.1 us (8%)
  between operations  17.4 us (8%)
  loops' own time  13 us (6%)
  other arithmetic  6.46 us (3%)
  starting transfers between devices  5.98 us (3%)
    ppermute x62, waiting for transfers between devices, passed_along(): return lax.ppermute(value, axis, pairs)  101 us
    all_gather x1, waiting for transfers between devices, shards(): all_gather(jnp.concatenate([key_states, value_states], axis=1), 'blk', ax...  35.6 us
    another operation x1, loops' own time, shards(): carry_state = lax.fori_loop(0, cycle_size - 1, key_turn, carry_state)  11.7 us
    dynamic_slice x16, local copies, waits for them, and re-layouts, key_step(): key_pos = block_order[source] * tok_rows + offsets  9.4 us
    dot_general x32, matrix products, mask_for(): jnp.dot(tile_rows, one_hot.T, preferred_element_type=jnp.float32) > 0.5  6.53 us
    ppermute x62, starting transfers between devices, passed_along(): return lax.ppermute(value, axis, pairs)  5.94 us
    dot_general x16, matrix products, softmax_update(): jnp.dot(weights.astype(jnp.bfloat16), value_sub, preferred_element_type=j...  4.83 us
  transfers between devices with their start and end apart: 63, of which 63 were waited for; matrix products, arithmetic and copies ran while one was open for 15% of the time, Pallas kernels for 0%

profile of v1, /device:TPU:0, one launch (start us, length us, event | category | flops | bytes accessed | tf_op | source)
XLA Modules:
  0.0 229.9 jit_solution(13838574433919404490)
XLA Ops:
  7.2 0.8 copy.83
  8.0 0.6 pad_maximum_fusion
  8.7 0.6 copy-done.3
  9.3 0.6 fusion.54
  13.1 0.7 fusion.74
  14.2 0.7 dynamic-slice_convert_fusion
  15.0 0.9 copy-done.1
  15.9 35.6 %all-gather.2.cloned.1.call-done = bf16[2048,256]{1,0:T(8,128)(2,1)} async-done(((bf16[128,256]{1,0:T(8,128)(2,1)}), bf16[2048,256]{1,0:T(8,128)(2,1)}) %all-gather.2.cloned.1.call-update) | async-done | bytes 1048592 | tf_op jit(solution)/shard_map/all_gather | solution.py:85
  51.4 1.3 fusion.53
  52.7 17.7 %while.47 = (s32[]{:T(128)}, f32[512]{0:T(512)S(1)}, f32[512]{0:T(512)S(1)}, f32[512,128]{1,0:T(8,128)S(1)}, s32[]{:T(128)}, /*index=5*/s32[16]{0:T(128)S(1)}, b...) while((s32[]{:T(128)}, f32[512]{0:T(512)S(1)}, ...), condition=%wide.region_4.5_spmd.clone, body=%wide.region_0.4_spmd.clone.sunk | while | flops 34965508 | bytes 1841459 | solution.py:108
  70.6 143.6 %while.48 = (s32[]{:T(128)}, bf16[128,128]{1,0:T(8,128)(2,1)S(1)}, bf16[128,128]{1,0:T(8,128)(2,1)S(1)}, f32[128,128]{1,0:T(8,128)S(1)}, f32[128,128]{1,0:T(8,12...) while((s32[]{:T(128)}, bf16[128,128]{1,0:T(8,128)(2,1)S(1)}, ...), condition=%wide.region_7.8_spmd.clone.clone, body=%wide.region_6.7_spmd.clone.clone.sunk | while | flops 85202960 | bytes 3711538 | solution.py:159
  74.2 1.4 collective-permute-start.3
  75.8 1.0 collective-permute-done
  77.1 3.0 %collective-permute-done.2 = f32[128,128]{1,0:T(8,128)S(1)} collective-permute-done((f32[128,128]{1,0:T(8,128)S(1)}, f32[128,128]{1,0:T(8,128)S(1)}, u32[]{:S(2)}, u32[]{:S(2)}) %collective-permute-start.2) | collective-permute-done | bytes 65568 | tf_op jit(solution)/shard_map/while/body/eval_jaxpr/ppermute | solution.py:13
  80.1 0.7 collective-permute-done.3
  83.5 1.1 collective-permute-start.3
  84.7 2.1 collective-permute-done
  87.2 2.4 %collective-permute-done.2 = f32[128,128]{1,0:T(8,128)S(1)} collective-permute-done((f32[128,128]{1,0:T(8,128)S(1)}, f32[128,128]{1,0:T(8,128)S(1)}, u32[]{:S(2)}, u32[]{:S(2)}) %collective-permute-start.2) | collective-permute-done | bytes 65568 | tf_op jit(solution)/shard_map/while/body/eval_jaxpr/ppermute | solution.py:13
  89.6 0.7 collective-permute-done.3
  93.3 3.1 %collective-permute-done = bf16[128,128]{1,0:T(8,128)(2,1)S(1)} collective-permute-done((bf16[128,128]{1,0:T(8,128)(2,1)S(1)}, bf16[128,128]{1,0:T(8,128)(2,1)S(1)}, u32[]{:S(2)}, u32[]{:S(2)}) %collective-permute-start) | collective-permute-done | bytes 32800 | tf_op jit(solution)/shard_map/while/body/eval_jaxpr/ppermute | solution.py:13
  96.7 2.4 %collective-permute-done.2 = f32[128,128]{1,0:T(8,128)S(1)} collective-permute-done((f32[128,128]{1,0:T(8,128)S(1)}, f32[128,128]{1,0:T(8,128)S(1)}, u32[]{:S(2)}, u32[]{:S(2)}) %collective-permute-start.2) | collective-permute-done | bytes 65568 | tf_op jit(solution)/shard_map/while/body/eval_jaxpr/ppermute | solution.py:13
  99.1 0.7 collective-permute-done.3
  102.8 3.1 %collective-permute-done = bf16[128,128]{1,0:T(8,128)(2,1)S(1)} collective-permute-done((bf16[128,128]{1,0:T(8,128)(2,1)S(1)}, bf16[128,128]{1,0:T(8,128)(2,1)S(1)}, u32[]{:S(2)}, u32[]{:S(2)}) %collective-permute-start) | collective-permute-done | bytes 32800 | tf_op jit(solution)/shard_map/while/body/eval_jaxpr/ppermute | solution.py:13
  106.2 2.4 %collective-permute-done.2 = f32[128,128]{1,0:T(8,128)S(1)} collective-permute-done((f32[128,128]{1,0:T(8,128)S(1)}, f32[128,128]{1,0:T(8,128)S(1)}, u32[]{:S(2)}, u32[]{:S(2)}) %collective-permute-start.2) | collective-permute-done | bytes 65568 | tf_op jit(solution)/shard_map/while/body/eval_jaxpr/ppermute | solution.py:13
  108.7 0.7 collective-permute-done.3
  112.3 3.1 %collective-permute-done = bf16[128,128]{1,0:T(8,128)(2,1)S(1)} collective-permute-done((bf16[128,128]{1,0:T(8,128)(2,1)S(1)}, bf16[128,128]{1,0:T(8,128)(2,1)S(1)}, u32[]{:S(2)}, u32[]{:S(2)}) %collective-permute-start) | collective-permute-done | bytes 32800 | tf_op jit(solution)/shard_map/while/body/eval_jaxpr/ppermute | solution.py:13
  115.8 2.4 %collective-permute-done.2 = f32[128,128]{1,0:T(8,128)S(1)} collective-permute-done((f32[128,128]{1,0:T(8,128)S(1)}, f32[128,128]{1,0:T(8,128)S(1)}, u32[]{:S(2)}, u32[]{:S(2)}) %collective-permute-start.2) | collective-permute-done | bytes 65568 | tf_op jit(solution)/shard_map/while/body/eval_jaxpr/ppermute | solution.py:13
  118.2 0.7 collective-permute-done.3
  121.9 3.1 %collective-permute-done = bf16[128,128]{1,0:T(8,128)(2,1)S(1)} collective-permute-done((bf16[128,128]{1,0:T(8,128)(2,1)S(1)}, bf16[128,128]{1,0:T(8,128)(2,1)S(1)}, u32[]{:S(2)}, u32[]{:S(2)}) %collective-permute-start) | collective-permute-done | bytes 32800 | tf_op jit(solution)/shard_map/while/body/eval_jaxpr/ppermute | solution.py:13
  125.3 2.4 %collective-permute-done.2 = f32[128,128]{1,0:T(8,128)S(1)} collective-permute-done((f32[128,128]{1,0:T(8,128)S(1)}, f32[128,128]{1,0:T(8,128)S(1)}, u32[]{:S(2)}, u32[]{:S(2)}) %collective-permute-start.2) | collective-permute-done | bytes 65568 | tf_op jit(solution)/shard_map/while/body/eval_jaxpr/ppermute | solution.py:13
  127.7 0.7 collective-permute-done.3
  131.4 3.1 %collective-permute-done = bf16[128,128]{1,0:T(8,128)(2,1)S(1)} collective-permute-done((bf16[128,128]{1,0:T(8,128)(2,1)S(1)}, bf16[128,128]{1,0:T(8,128)(2,1)S(1)}, u32[]{:S(2)}, u32[]{:S(2)}) %collective-permute-start) | collective-permute-done | bytes 32800 | tf_op jit(solution)/shard_map/while/body/eval_jaxpr/ppermute | solution.py:13
  134.8 2.4 %collective-permute-done.2 = f32[128,128]{1,0:T(8,128)S(1)} collective-permute-done((f32[128,128]{1,0:T(8,128)S(1)}, f32[128,128]{1,0:T(8,128)S(1)}, u32[]{:S(2)}, u32[]{:S(2)}) %collective-permute-start.2) | collective-permute-done | bytes 65568 | tf_op jit(solution)/shard_map/while/body/eval_jaxpr/ppermute | solution.py:13
  137.3 0.7 collective-permute-done.3
  140.9 3.1 %collective-permute-done = bf16[128,128]{1,0:T(8,128)(2,1)S(1)} collective-permute-done((bf16[128,128]{1,0:T(8,128)(2,1)S(1)}, bf16[128,128]{1,0:T(8,128)(2,1)S(1)}, u32[]{:S(2)}, u32[]{:S(2)}) %collective-permute-start) | collective-permute-done | bytes 32800 | tf_op jit(solution)/shard_map/while/body/eval_jaxpr/ppermute | solution.py:13
  144.3 2.4 %collective-permute-done.2 = f32[128,128]{1,0:T(8,128)S(1)} collective-permute-done((f32[128,128]{1,0:T(8,128)S(1)}, f32[128,128]{1,0:T(8,128)S(1)}, u32[]{:S(2)}, u32[]{:S(2)}) %collective-permute-start.2) | collective-permute-done | bytes 65568 | tf_op jit(solution)/shard_map/while/body/eval_jaxpr/ppermute | solution.py:13
  146.8 0.7 collective-permute-done.3
  150.5 3.1 %collective-permute-done = bf16[128,128]{1,0:T(8,128)(2,1)S(1)} collective-permute-done((bf16[128,128]{1,0:T(8,128)(2,1)S(1)}, bf16[128,128]{1,0:T(8,128)(2,1)S(1)}, u32[]{:S(2)}, u32[]{:S(2)}) %collective-permute-start) | collective-permute-done | bytes 32800 | tf_op jit(solution)/shard_map/while/body/eval_jaxpr/ppermute | solution.py:13
  153.9 2.4 %collective-permute-done.2 = f32[128,128]{1,0:T(8,128)S(1)} collective-permute-done((f32[128,128]{1,0:T(8,128)S(1)}, f32[128,128]{1,0:T(8,128)S(1)}, u32[]{:S(2)}, u32[]{:S(2)}) %collective-permute-start.2) | collective-permute-done | bytes 65568 | tf_op jit(solution)/shard_map/while/body/eval_jaxpr/ppermute | solution.py:13
  156.3 0.7 collective-permute-done.3
  160.0 3.1 %collective-permute-done = bf16[128,128]{1,0:T(8,128)(2,1)S(1)} collective-permute-done((bf16[128,128]{1,0:T(8,128)(2,1)S(1)}, bf16[128,128]{1,0:T(8,128)(2,1)S(1)}, u32[]{:S(2)}, u32[]{:S(2)}) %collective-permute-start) | collective-permute-done | bytes 32800 | tf_op jit(solution)/shard_map/while/body/eval_jaxpr/ppermute | solution.py:13
  163.4 2.4 %collective-permute-done.2 = f32[128,128]{1,0:T(8,128)S(1)} collective-permute-done((f32[128,128]{1,0:T(8,128)S(1)}, f32[128,128]{1,0:T(8,128)S(1)}, u32[]{:S(2)}, u32[]{:S(2)}) %collective-permute-start.2) | collective-permute-done | bytes 65568 | tf_op jit(solution)/shard_map/while/body/eval_jaxpr/ppermute | solution.py:13
  165.8 0.7 collective-permute-done.3
  169.5 3.1 %collective-permute-done = bf16[128,128]{1,0:T(8,128)(2,1)S(1)} collective-permute-done((bf16[128,128]{1,0:T(8,128)(2,1)S(1)}, bf16[128,128]{1,0:T(8,128)(2,1)S(1)}, u32[]{:S(2)}, u32[]{:S(2)}) %collective-permute-start) | collective-permute-done | bytes 32800 | tf_op jit(solution)/shard_map/while/body/eval_jaxpr/ppermute | solution.py:13
  172.9 2.4 %collective-permute-done.2 = f32[128,128]{1,0:T(8,128)S(1)} collective-permute-done((f32[128,128]{1,0:T(8,128)S(1)}, f32[128,128]{1,0:T(8,128)S(1)}, u32[]{:S(2)}, u32[]{:S(2)}) %collective-permute-start.2) | collective-permute-done | bytes 65568 | tf_op jit(solution)/shard_map/while/body/eval_jaxpr/ppermute | solution.py:13
  175.4 0.7 collective-permute-done.3
  179.1 3.1 %collective-permute-done = bf16[128,128]{1,0:T(8,128)(2,1)S(1)} collective-permute-done((bf16[128,128]{1,0:T(8,128)(2,1)S(1)}, bf16[128,128]{1,0:T(8,128)(2,1)S(1)}, u32[]{:S(2)}, u32[]{:S(2)}) %collective-permute-start) | collective-permute-done | bytes 32800 | tf_op jit(solution)/shard_map/while/body/eval_jaxpr/ppermute | solution.py:13
  182.5 2.4 %collective-permute-done.2 = f32[128,128]{1,0:T(8,128)S(1)} collective-permute-done((f32[128,128]{1,0:T(8,128)S(1)}, f32[128,128]{1,0:T(8,128)S(1)}, u32[]{:S(2)}, u32[]{:S(2)}) %collective-permute-start.2) | collective-permute-done | bytes 65568 | tf_op jit(solution)/shard_map/while/body/eval_jaxpr/ppermute | solution.py:13
  184.9 0.7 collective-permute-done.3
  188.6 3.1 %collective-permute-done = bf16[128,128]{1,0:T(8,128)(2,1)S(1)} collective-permute-done((bf16[128,128]{1,0:T(8,128)(2,1)S(1)}, bf16[128,128]{1,0:T(8,128)(2,1)S(1)}, u32[]{:S(2)}, u32[]{:S(2)}) %collective-permute-start) | collective-permute-done | bytes 32800 | tf_op jit(solution)/shard_map/while/body/eval_jaxpr/ppermute | solution.py:13
  192.0 2.4 %collective-permute-done.2 = f32[128,128]{1,0:T(8,128)S(1)} collective-permute-done((f32[128,128]{1,0:T(8,128)S(1)}, f32[128,128]{1,0:T(8,128)S(1)}, u32[]{:S(2)}, u32[]{:S(2)}) %collective-permute-start.2) | collective-permute-done | bytes 65568 | tf_op jit(solution)/shard_map/while/body/eval_jaxpr/ppermute | solution.py:13
  194.4 0.7 collective-permute-done.3
  198.1 3.1 %collective-permute-done = bf16[128,128]{1,0:T(8,128)(2,1)S(1)} collective-permute-done((bf16[128,128]{1,0:T(8,128)(2,1)S(1)}, bf16[128,128]{1,0:T(8,128)(2,1)S(1)}, u32[]{:S(2)}, u32[]{:S(2)}) %collective-permute-start) | collective-permute-done | bytes 32800 | tf_op jit(solution)/shard_map/while/body/eval_jaxpr/ppermute | solution.py:13
  201.5 2.4 %collective-permute-done.2 = f32[128,128]{1,0:T(8,128)S(1)} collective-permute-done((f32[128,128]{1,0:T(8,128)S(1)}, f32[128,128]{1,0:T(8,128)S(1)}, u32[]{:S(2)}, u32[]{:S(2)}) %collective-permute-start.2) | collective-permute-done | bytes 65568 | tf_op jit(solution)/shard_map/while/body/eval_jaxpr/ppermute | solution.py:13
  204.0 0.7 collective-permute-done.3
  207.7 3.1 %collective-permute-done = bf16[128,128]{1,0:T(8,128)(2,1)S(1)} collective-permute-done((bf16[128,128]{1,0:T(8,128)(2,1)S(1)}, bf16[128,128]{1,0:T(8,128)(2,1)S(1)}, u32[]{:S(2)}, u32[]{:S(2)}) %collective-permute-start) | collective-permute-done | bytes 32800 | tf_op jit(solution)/shard_map/while/body/eval_jaxpr/ppermute | solution.py:13
  211.1 2.4 %collective-permute-done.2 = f32[128,128]{1,0:T(8,128)S(1)} collective-permute-done((f32[128,128]{1,0:T(8,128)S(1)}, f32[128,128]{1,0:T(8,128)S(1)}, u32[]{:S(2)}, u32[]{:S(2)}) %collective-permute-start.2) | collective-permute-done | bytes 65568 | tf_op jit(solution)/shard_map/while/body/eval_jaxpr/ppermute | solution.py:13
  213.5 0.7 collective-permute-done.3
  215.4 0.7 copy.41
  216.2 0.7 copy.40
  216.9 4.2 %collective-permute-done.5 = f32[128,128]{1,0:T(8,128)S(1)} collective-permute-done((f32[128,128]{1,0:T(8,128)S(1)}, f32[128,128]{1,0:T(8,128)S(1)}, u32[]{:S(2)}, u32[]{:S(2)}) %collective-permute-start.5) | collective-permute-done | bytes 65568 | tf_op jit(solution)/shard_map/ppermute | solution.py:13
  221.1 0.7 collective-permute-done.4
  221.8 0.6 copy.85
  222.5 0.6 copy.86
  (492 shorter events, 57.3 us)
Async XLA Ops:
  7.2 7.8 %copy-start = (bf16[128,512]{1,0:T(8,128)(2,1)S(1)}, bf16[128,512]{1,0:T(8,128)(2,1)}, u32[]{:S(2)}) copy-start(bf16[128,512]{1,0:T(8,128)(2,1)} %param.10) | copy-start | bytes 393220
  7.2 44.2 %all-gather.2.cloned.1.call-start = ((), (), s32[]{:S(2)}) async-start(), calls=%async_computation | async-start | bytes 1114112 | tf_op jit(solution)/shard_map/all_gather | solution.py:85
  70.7 6.1 %collective-permute-start = (bf16[128,128]{1,0:T(8,128)(2,1)S(1)}, bf16[128,128]{1,0:T(8,128)(2,1)S(1)}, u32[]{:S(2)}, u32[]{:S(2)}) collective-permute-start(bf16[128,128]{1,0:T(8,128)(2,1)S(1)} %copy.67), channel_id=1, source_target_pairs={{0,1},{1,2},{2,3},{3,4},{4,5},{5,6},{6,7},{7,8},{8,9},{9,10},{10,1... | collective-permute-start | bytes 98312 | tf_op jit(solution)/shard_map/while/body/eval_jaxpr/ppermute | solution.py:13
  71.0 6.1 %collective-permute-start.1 = (bf16[128,128]{1,0:T(8,128)(2,1)S(1)}, bf16[128,128]{1,0:T(8,128)(2,1)S(1)}, u32[]{:S(2)}, u32[]{:S(2)}) collective-permute-start(bf16[128,128]{1,0:T(8,128)(2,1)S(1)} %copy.68), channel_id=1, source_target_pairs={{0,1},{1,2},{2,3},{3,4},{4,5},{5,6},{6,7},{7,8},{8,9},{9,10},{10,1... | collective-permute-start | bytes 98312 | tf_op jit(solution)/shard_map/while/body/eval_jaxpr/ppermute | solution.py:13
  73.6 6.4 %collective-permute-start.2 = (f32[128,128]{1,0:T(8,128)S(1)}, f32[128,128]{1,0:T(8,128)S(1)}, u32[]{:S(2)}, u32[]{:S(2)}) collective-permute-start(f32[128,128]{1,0:T(8,128)S(1)} %fusion.123), channel_id=1, source_target_pairs={{0,1},{1,2},{2,3},{3,4},{4,5},{5,6},{6,7},{7,8},{8,9},{9,10},{10,1... | collective-permute-start | bytes 196616 | tf_op jit(solution)/shard_map/while/body/eval_jaxpr/ppermute | solution.py:13
  74.2 6.6 %collective-permute-start.3 = (f32[128,128]{1,0:T(8,128)S(1)}, f32[128,128]{1,0:T(8,128)S(1)}, u32[]{:S(2)}, u32[]{:S(2)}) collective-permute-start(f32[128,128]{1,0:T(8,128)S(1)} %convolution_add_fusion.6), channel_id=1, source_target_pairs={{0,1},{1,2},{2,3},{3,4},{4,5},{5,6},{6,7},{7,8},{8,9},{9,10},{10,1... | collective-permute-start | bytes 196616 | tf_op jit(solution)/shard_map/while/body/eval_jaxpr/ppermute | solution.py:13
  80.8 6.0 %collective-permute-start = (bf16[128,128]{1,0:T(8,128)(2,1)S(1)}, bf16[128,128]{1,0:T(8,128)(2,1)S(1)}, u32[]{:S(2)}, u32[]{:S(2)}) collective-permute-start(bf16[128,128]{1,0:T(8,128)(2,1)S(1)} %copy.67), channel_id=1, source_target_pairs={{0,1},{1,2},{2,3},{3,4},{4,5},{5,6},{6,7},{7,8},{8,9},{9,10},{10,1... | collective-permute-start | bytes 98312 | tf_op jit(solution)/shard_map/while/body/eval_jaxpr/ppermute | solution.py:13
  80.8 6.4 %collective-permute-start.1 = (bf16[128,128]{1,0:T(8,128)(2,1)S(1)}, bf16[128,128]{1,0:T(8,128)(2,1)S(1)}, u32[]{:S(2)}, u32[]{:S(2)}) collective-permute-start(bf16[128,128]{1,0:T(8,128)(2,1)S(1)} %copy.68), channel_id=1, source_target_pairs={{0,1},{1,2},{2,3},{3,4},{4,5},{5,6},{6,7},{7,8},{8,9},{9,10},{10,1... | collective-permute-start | bytes 98312 | tf_op jit(solution)/shard_map/while/body/eval_jaxpr/ppermute | solution.py:13
  83.2 6.4 %collective-permute-start.2 = (f32[128,128]{1,0:T(8,128)S(1)}, f32[128,128]{1,0:T(8,128)S(1)}, u32[]{:S(2)}, u32[]{:S(2)}) collective-permute-start(f32[128,128]{1,0:T(8,128)S(1)} %fusion.123), channel_id=1, source_target_pairs={{0,1},{1,2},{2,3},{3,4},{4,5},{5,6},{6,7},{7,8},{8,9},{9,10},{10,1... | collective-permute-start | bytes 196616 | tf_op jit(solution)/shard_map/while/body/eval_jaxpr/ppermute | solution.py:13
  83.5 6.8 %collective-permute-start.3 = (f32[128,128]{1,0:T(8,128)S(1)}, f32[128,128]{1,0:T(8,128)S(1)}, u32[]{:S(2)}, u32[]{:S(2)}) collective-permute-start(f32[128,128]{1,0:T(8,128)S(1)} %convolution_add_fusion.6), channel_id=1, source_target_pairs={{0,1},{1,2},{2,3},{3,4},{4,5},{5,6},{6,7},{7,8},{8,9},{9,10},{10,1... | collective-permute-start | bytes 196616 | tf_op jit(solution)/shard_map/while/body/eval_jaxpr/ppermute | solution.py:13
  90.3 6.0 %collective-permute-start = (bf16[128,128]{1,0:T(8,128)(2,1)S(1)}, bf16[128,128]{1,0:T(8,128)(2,1)S(1)}, u32[]{:S(2)}, u32[]{:S(2)}) collective-permute-start(bf16[128,128]{1,0:T(8,128)(2,1)S(1)} %copy.67), channel_id=1, source_target_pairs={{0,1},{1,2},{2,3},{3,4},{4,5},{5,6},{6,7},{7,8},{8,9},{9,10},{10,1... | collective-permute-start | bytes 98312 | tf_op jit(solution)/shard_map/while/body/eval_jaxpr/ppermute | solution.py:13
  90.3 6.4 %collective-permute-start.1 = (bf16[128,128]{1,0:T(8,128)(2,1)S(1)}, bf16[128,128]{1,0:T(8,128)(2,1)S(1)}, u32[]{:S(2)}, u32[]{:S(2)}) collective-permute-start(bf16[128,128]{1,0:T(8,128)(2,1)S(1)} %copy.68), channel_id=1, source_target_pairs={{0,1},{1,2},{2,3},{3,4},{4,5},{5,6},{6,7},{7,8},{8,9},{9,10},{10,1... | collective-permute-start | bytes 98312 | tf_op jit(solution)/shard_map/while/body/eval_jaxpr/ppermute | solution.py:13
  92.7 6.4 %collective-permute-start.2 = (f32[128,128]{1,0:T(8,128)S(1)}, f32[128,128]{1,0:T(8,128)S(1)}, u32[]{:S(2)}, u32[]{:S(2)}) collective-permute-start(f32[128,128]{1,0:T(8,128)S(1)} %fusion.123), channel_id=1, source_target_pairs={{0,1},{1,2},{2,3},{3,4},{4,5},{5,6},{6,7},{7,8},{8,9},{9,10},{10,1... | collective-permute-start | bytes 196616 | tf_op jit(solution)/shard_map/while/body/eval_jaxpr/ppermute | solution.py:13
  93.0 6.8 %collective-permute-start.3 = (f32[128,128]{1,0:T(8,128)S(1)}, f32[128,128]{1,0:T(8,128)S(1)}, u32[]{:S(2)}, u32[]{:S(2)}) collective-permute-start(f32[128,128]{1,0:T(8,128)S(1)} %convolution_add_fusion.6), channel_id=1, source_target_pairs={{0,1},{1,2},{2,3},{3,4},{4,5},{5,6},{6,7},{7,8},{8,9},{9,10},{10,1... | collective-permute-start | bytes 196616 | tf_op jit(solution)/shard_map/while/body/eval_jaxpr/ppermute | solution.py:13
  99.8 6.0 %collective-permute-start = (bf16[128,128]{1,0:T(8,128)(2,1)S(1)}, bf16[128,128]{1,0:T(8,128)(2,1)S(1)}, u32[]{:S(2)}, u32[]{:S(2)}) collective-permute-start(bf16[128,128]{1,0:T(8,128)(2,1)S(1)} %copy.67), channel_id=1, source_target_pairs={{0,1},{1,2},{2,3},{3,4},{4,5},{5,6},{6,7},{7,8},{8,9},{9,10},{10,1... | collective-permute-start | bytes 98312 | tf_op jit(solution)/shard_map/while/body/eval_jaxpr/ppermute | solution.py:13
  99.8 6.4 %collective-permute-start.1 = (bf16[128,128]{1,0:T(8,128)(2,1)S(1)}, bf16[128,128]{1,0:T(8,128)(2,1)S(1)}, u32[]{:S(2)}, u32[]{:S(2)}) collective-permute-start(bf16[128,128]{1,0:T(8,128)(2,1)S(1)} %copy.68), channel_id=1, source_target_pairs={{0,1},{1,2},{2,3},{3,4},{4,5},{5,6},{6,7},{7,8},{8,9},{9,10},{10,1... | collective-permute-start | bytes 98312 | tf_op jit(solution)/shard_map/while/body/eval_jaxpr/ppermute | solution.py:13
  102.2 6.4 %collective-permute-start.2 = (f32[128,128]{1,0:T(8,128)S(1)}, f32[128,128]{1,0:T(8,128)S(1)}, u32[]{:S(2)}, u32[]{:S(2)}) collective-permute-start(f32[128,128]{1,0:T(8,128)S(1)} %fusion.123), channel_id=1, source_target_pairs={{0,1},{1,2},{2,3},{3,4},{4,5},{5,6},{6,7},{7,8},{8,9},{9,10},{10,1... | collective-permute-start | bytes 196616 | tf_op jit(solution)/shard_map/while/body/eval_jaxpr/ppermute | solution.py:13
  102.5 6.8 %collective-permute-start.3 = (f32[128,128]{1,0:T(8,128)S(1)}, f32[128,128]{1,0:T(8,128)S(1)}, u32[]{:S(2)}, u32[]{:S(2)}) collective-permute-start(f32[128,128]{1,0:T(8,128)S(1)} %convolution_add_fusion.6), channel_id=1, source_target_pairs={{0,1},{1,2},{2,3},{3,4},{4,5},{5,6},{6,7},{7,8},{8,9},{9,10},{10,1... | collective-permute-start | bytes 196616 | tf_op jit(solution)/shard_map/while/body/eval_jaxpr/ppermute | solution.py:13
  109.4 6.0 %collective-permute-start = (bf16[128,128]{1,0:T(8,128)(2,1)S(1)}, bf16[128,128]{1,0:T(8,128)(2,1)S(1)}, u32[]{:S(2)}, u32[]{:S(2)}) collective-permute-start(bf16[128,128]{1,0:T(8,128)(2,1)S(1)} %copy.67), channel_id=1, source_target_pairs={{0,1},{1,2},{2,3},{3,4},{4,5},{5,6},{6,7},{7,8},{8,9},{9,10},{10,1... | collective-permute-start | bytes 98312 | tf_op jit(solution)/shard_map/while/body/eval_jaxpr/ppermute | solution.py:13
  109.4 6.4 %collective-permute-start.1 = (bf16[128,128]{1,0:T(8,128)(2,1)S(1)}, bf16[128,128]{1,0:T(8,128)(2,1)S(1)}, u32[]{:S(2)}, u32[]{:S(2)}) collective-permute-start(bf16[128,128]{1,0:T(8,128)(2,1)S(1)} %copy.68), channel_id=1, source_target_pairs={{0,1},{1,2},{2,3},{3,4},{4,5},{5,6},{6,7},{7,8},{8,9},{9,10},{10,1... | collective-permute-start | bytes 98312 | tf_op jit(solution)/shard_map/while/body/eval_jaxpr/ppermute | solution.py:13
  111.7 6.4 %collective-permute-start.2 = (f32[128,128]{1,0:T(8,128)S(1)}, f32[128,128]{1,0:T(8,128)S(1)}, u32[]{:S(2)}, u32[]{:S(2)}) collective-permute-start(f32[128,128]{1,0:T(8,128)S(1)} %fusion.123), channel_id=1, source_target_pairs={{0,1},{1,2},{2,3},{3,4},{4,5},{5,6},{6,7},{7,8},{8,9},{9,10},{10,1... | collective-permute-start | bytes 196616 | tf_op jit(solution)/shard_map/while/body/eval_jaxpr/ppermute | solution.py:13
  112.1 6.8 %collective-permute-start.3 = (f32[128,128]{1,0:T(8,128)S(1)}, f32[128,128]{1,0:T(8,128)S(1)}, u32[]{:S(2)}, u32[]{:S(2)}) collective-permute-start(f32[128,128]{1,0:T(8,128)S(1)} %convolution_add_fusion.6), channel_id=1, source_target_pairs={{0,1},{1,2},{2,3},{3,4},{4,5},{5,6},{6,7},{7,8},{8,9},{9,10},{10,1... | collective-permute-start | bytes 196616 | tf_op jit(solution)/shard_map/while/body/eval_jaxpr/ppermute | solution.py:13
  118.9 6.0 %collective-permute-start = (bf16[128,128]{1,0:T(8,128)(2,1)S(1)}, bf16[128,128]{1,0:T(8,128)(2,1)S(1)}, u32[]{:S(2)}, u32[]{:S(2)}) collective-permute-start(bf16[128,128]{1,0:T(8,128)(2,1)S(1)} %copy.67), channel_id=1, source_target_pairs={{0,1},{1,2},{2,3},{3,4},{4,5},{5,6},{6,7},{7,8},{8,9},{9,10},{10,1... | collective-permute-start | bytes 98312 | tf_op jit(solution)/shard_map/while/body/eval_jaxpr/ppermute | solution.py:13
  118.9 6.4 %collective-permute-start.1 = (bf16[128,128]{1,0:T(8,128)(2,1)S(1)}, bf16[128,128]{1,0:T(8,128)(2,1)S(1)}, u32[]{:S(2)}, u32[]{:S(2)}) collective-permute-start(bf16[128,128]{1,0:T(8,128)(2,1)S(1)} %copy.68), channel_id=1, source_target_pairs={{0,1},{1,2},{2,3},{3,4},{4,5},{5,6},{6,7},{7,8},{8,9},{9,10},{10,1... | collective-permute-start | bytes 98312 | tf_op jit(solution)/shard_map/while/body/eval_jaxpr/ppermute | solution.py:13
  121.3 6.4 %collective-permute-start.2 = (f32[128,128]{1,0:T(8,128)S(1)}, f32[128,128]{1,0:T(8,128)S(1)}, u32[]{:S(2)}, u32[]{:S(2)}) collective-permute-start(f32[128,128]{1,0:T(8,128)S(1)} %fusion.123), channel_id=1, source_target_pairs={{0,1},{1,2},{2,3},{3,4},{4,5},{5,6},{6,7},{7,8},{8,9},{9,10},{10,1... | collective-permute-start | bytes 196616 | tf_op jit(solution)/shard_map/while/body/eval_jaxpr/ppermute | solution.py:13
  121.6 6.8 %collective-permute-start.3 = (f32[128,128]{1,0:T(8,128)S(1)}, f32[128,128]{1,0:T(8,128)S(1)}, u32[]{:S(2)}, u32[]{:S(2)}) collective-permute-start(f32[128,128]{1,0:T(8,128)S(1)} %convolution_add_fusion.6), channel_id=1, source_target_pairs={{0,1},{1,2},{2,3},{3,4},{4,5},{5,6},{6,7},{7,8},{8,9},{9,10},{10,1... | collective-permute-start | bytes 196616 | tf_op jit(solution)/shard_map/while/body/eval_jaxpr/ppermute | solution.py:13
  128.4 6.0 %collective-permute-start = (bf16[128,128]{1,0:T(8,128)(2,1)S(1)}, bf16[128,128]{1,0:T(8,128)(2,1)S(1)}, u32[]{:S(2)}, u32[]{:S(2)}) collective-permute-start(bf16[128,128]{1,0:T(8,128)(2,1)S(1)} %copy.67), channel_id=1, source_target_pairs={{0,1},{1,2},{2,3},{3,4},{4,5},{5,6},{6,7},{7,8},{8,9},{9,10},{10,1... | collective-permute-start | bytes 98312 | tf_op jit(solution)/shard_map/while/body/eval_jaxpr/ppermute | solution.py:13
  128.4 6.4 %collective-permute-start.1 = (bf16[128,128]{1,0:T(8,128)(2,1)S(1)}, bf16[128,128]{1,0:T(8,128)(2,1)S(1)}, u32[]{:S(2)}, u32[]{:S(2)}) collective-permute-start(bf16[128,128]{1,0:T(8,128)(2,1)S(1)} %copy.68), channel_id=1, source_target_pairs={{0,1},{1,2},{2,3},{3,4},{4,5},{5,6},{6,7},{7,8},{8,9},{9,10},{10,1... | collective-permute-start | bytes 98312 | tf_op jit(solution)/shard_map/while/body/eval_jaxpr/ppermute | solution.py:13
  130.8 6.4 %collective-permute-start.2 = (f32[128,128]{1,0:T(8,128)S(1)}, f32[128,128]{1,0:T(8,128)S(1)}, u32[]{:S(2)}, u32[]{:S(2)}) collective-permute-start(f32[128,128]{1,0:T(8,128)S(1)} %fusion.123), channel_id=1, source_target_pairs={{0,1},{1,2},{2,3},{3,4},{4,5},{5,6},{6,7},{7,8},{8,9},{9,10},{10,1... | collective-permute-start | bytes 196616 | tf_op jit(solution)/shard_map/while/body/eval_jaxpr/ppermute | solution.py:13
  131.1 6.8 %collective-permute-start.3 = (f32[128,128]{1,0:T(8,128)S(1)}, f32[128,128]{1,0:T(8,128)S(1)}, u32[]{:S(2)}, u32[]{:S(2)}) collective-permute-start(f32[128,128]{1,0:T(8,128)S(1)} %convolution_add_fusion.6), channel_id=1, source_target_pairs={{0,1},{1,2},{2,3},{3,4},{4,5},{5,6},{6,7},{7,8},{8,9},{9,10},{10,1... | collective-permute-start | bytes 196616 | tf_op jit(solution)/shard_map/while/body/eval_jaxpr/ppermute | solution.py:13
  138.0 6.0 %collective-permute-start = (bf16[128,128]{1,0:T(8,128)(2,1)S(1)}, bf16[128,128]{1,0:T(8,128)(2,1)S(1)}, u32[]{:S(2)}, u32[]{:S(2)}) collective-permute-start(bf16[128,128]{1,0:T(8,128)(2,1)S(1)} %copy.67), channel_id=1, source_target_pairs={{0,1},{1,2},{2,3},{3,4},{4,5},{5,6},{6,7},{7,8},{8,9},{9,10},{10,1... | collective-permute-start | bytes 98312 | tf_op jit(solution)/shard_map/while/body/eval_jaxpr/ppermute | solution.py:13
  138.0 6.4 %collective-permute-start.1 = (bf16[128,128]{1,0:T(8,128)(2,1)S(1)}, bf16[128,128]{1,0:T(8,128)(2,1)S(1)}, u32[]{:S(2)}, u32[]{:S(2)}) collective-permute-start(bf16[128,128]{1,0:T(8,128)(2,1)S(1)} %copy.68), channel_id=1, source_target_pairs={{0,1},{1,2},{2,3},{3,4},{4,5},{5,6},{6,7},{7,8},{8,9},{9,10},{10,1... | collective-permute-start | bytes 98312 | tf_op jit(solution)/shard_map/while/body/eval_jaxpr/ppermute | solution.py:13
  140.3 6.4 %collective-permute-start.2 = (f32[128,128]{1,0:T(8,128)S(1)}, f32[128,128]{1,0:T(8,128)S(1)}, u32[]{:S(2)}, u32[]{:S(2)}) collective-permute-start(f32[128,128]{1,0:T(8,128)S(1)} %fusion.123), channel_id=1, source_target_pairs={{0,1},{1,2},{2,3},{3,4},{4,5},{5,6},{6,7},{7,8},{8,9},{9,10},{10,1... | collective-permute-start | bytes 196616 | tf_op jit(solution)/shard_map/while/body/eval_jaxpr/ppermute | solution.py:13
  140.6 6.8 %collective-permute-start.3 = (f32[128,128]{1,0:T(8,128)S(1)}, f32[128,128]{1,0:T(8,128)S(1)}, u32[]{:S(2)}, u32[]{:S(2)}) collective-permute-start(f32[128,128]{1,0:T(8,128)S(1)} %convolution_add_fusion.6), channel_id=1, source_target_pairs={{0,1},{1,2},{2,3},{3,4},{4,5},{5,6},{6,7},{7,8},{8,9},{9,10},{10,1... | collective-permute-start | bytes 196616 | tf_op jit(solution)/shard_map/while/body/eval_jaxpr/ppermute | solution.py:13
  147.5 6.0 %collective-permute-start = (bf16[128,128]{1,0:T(8,128)(2,1)S(1)}, bf16[128,128]{1,0:T(8,128)(2,1)S(1)}, u32[]{:S(2)}, u32[]{:S(2)}) collective-permute-start(bf16[128,128]{1,0:T(8,128)(2,1)S(1)} %copy.67), channel_id=1, source_target_pairs={{0,1},{1,2},{2,3},{3,4},{4,5},{5,6},{6,7},{7,8},{8,9},{9,10},{10,1... | collective-permute-start | bytes 98312 | tf_op jit(solution)/shard_map/while/body/eval_jaxpr/ppermute | solution.py:13
  147.5 6.4 %collective-permute-start.1 = (bf16[128,128]{1,0:T(8,128)(2,1)S(1)}, bf16[128,128]{1,0:T(8,128)(2,1)S(1)}, u32[]{:S(2)}, u32[]{:S(2)}) collective-permute-start(bf16[128,128]{1,0:T(8,128)(2,1)S(1)} %copy.68), channel_id=1, source_target_pairs={{0,1},{1,2},{2,3},{3,4},{4,5},{5,6},{6,7},{7,8},{8,9},{9,10},{10,1... | collective-permute-start | bytes 98312 | tf_op jit(solution)/shard_map/while/body/eval_jaxpr/ppermute | solution.py:13
  149.9 6.4 %collective-permute-start.2 = (f32[128,128]{1,0:T(8,128)S(1)}, f32[128,128]{1,0:T(8,128)S(1)}, u32[]{:S(2)}, u32[]{:S(2)}) collective-permute-start(f32[128,128]{1,0:T(8,128)S(1)} %fusion.123), channel_id=1, source_target_pairs={{0,1},{1,2},{2,3},{3,4},{4,5},{5,6},{6,7},{7,8},{8,9},{9,10},{10,1... | collective-permute-start | bytes 196616 | tf_op jit(solution)/shard_map/while/body/eval_jaxpr/ppermute | solution.py:13
  150.2 6.8 %collective-permute-start.3 = (f32[128,128]{1,0:T(8,128)S(1)}, f32[128,128]{1,0:T(8,128)S(1)}, u32[]{:S(2)}, u32[]{:S(2)}) collective-permute-start(f32[128,128]{1,0:T(8,128)S(1)} %convolution_add_fusion.6), channel_id=1, source_target_pairs={{0,1},{1,2},{2,3},{3,4},{4,5},{5,6},{6,7},{7,8},{8,9},{9,10},{10,1... | collective-permute-start | bytes 196616 | tf_op jit(solution)/shard_map/while/body/eval_jaxpr/ppermute | solution.py:13
  157.0 6.0 %collective-permute-start = (bf16[128,128]{1,0:T(8,128)(2,1)S(1)}, bf16[128,128]{1,0:T(8,128)(2,1)S(1)}, u32[]{:S(2)}, u32[]{:S(2)}) collective-permute-start(bf16[128,128]{1,0:T(8,128)(2,1)S(1)} %copy.67), channel_id=1, source_target_pairs={{0,1},{1,2},{2,3},{3,4},{4,5},{5,6},{6,7},{7,8},{8,9},{9,10},{10,1... | collective-permute-start | bytes 98312 | tf_op jit(solution)/shard_map/while/body/eval_jaxpr/ppermute | solution.py:13
  157.0 6.4 %collective-permute-start.1 = (bf16[128,128]{1,0:T(8,128)(2,1)S(1)}, bf16[128,128]{1,0:T(8,128)(2,1)S(1)}, u32[]{:S(2)}, u32[]{:S(2)}) collective-permute-start(bf16[128,128]{1,0:T(8,128)(2,1)S(1)} %copy.68), channel_id=1, source_target_pairs={{0,1},{1,2},{2,3},{3,4},{4,5},{5,6},{6,7},{7,8},{8,9},{9,10},{10,1... | collective-permute-start | bytes 98312 | tf_op jit(solution)/shard_map/while/body/eval_jaxpr/ppermute | solution.py:13
  159.4 6.4 %collective-permute-start.2 = (f32[128,128]{1,0:T(8,128)S(1)}, f32[128,128]{1,0:T(8,128)S(1)}, u32[]{:S(2)}, u32[]{:S(2)}) collective-permute-start(f32[128,128]{1,0:T(8,128)S(1)} %fusion.123), channel_id=1, source_target_pairs={{0,1},{1,2},{2,3},{3,4},{4,5},{5,6},{6,7},{7,8},{8,9},{9,10},{10,1... | collective-permute-start | bytes 196616 | tf_op jit(solution)/shard_map/while/body/eval_jaxpr/ppermute | solution.py:13
  159.7 6.8 %collective-permute-start.3 = (f32[128,128]{1,0:T(8,128)S(1)}, f32[128,128]{1,0:T(8,128)S(1)}, u32[]{:S(2)}, u32[]{:S(2)}) collective-permute-start(f32[128,128]{1,0:T(8,128)S(1)} %convolution_add_fusion.6), channel_id=1, source_target_pairs={{0,1},{1,2},{2,3},{3,4},{4,5},{5,6},{6,7},{7,8},{8,9},{9,10},{10,1... | collective-permute-start | bytes 196616 | tf_op jit(solution)/shard_map/while/body/eval_jaxpr/ppermute | solution.py:13
  166.6 6.0 %collective-permute-start = (bf16[128,128]{1,0:T(8,128)(2,1)S(1)}, bf16[128,128]{1,0:T(8,128)(2,1)S(1)}, u32[]{:S(2)}, u32[]{:S(2)}) collective-permute-start(bf16[128,128]{1,0:T(8,128)(2,1)S(1)} %copy.67), channel_id=1, source_target_pairs={{0,1},{1,2},{2,3},{3,4},{4,5},{5,6},{6,7},{7,8},{8,9},{9,10},{10,1... | collective-permute-start | bytes 98312 | tf_op jit(solution)/shard_map/while/body/eval_jaxpr/ppermute | solution.py:13
  166.6 6.4 %collective-permute-start.1 = (bf16[128,128]{1,0:T(8,128)(2,1)S(1)}, bf16[128,128]{1,0:T(8,128)(2,1)S(1)}, u32[]{:S(2)}, u32[]{:S(2)}) collective-permute-start(bf16[128,128]{1,0:T(8,128)(2,1)S(1)} %copy.68), channel_id=1, source_target_pairs={{0,1},{1,2},{2,3},{3,4},{4,5},{5,6},{6,7},{7,8},{8,9},{9,10},{10,1... | collective-permute-start | bytes 98312 | tf_op jit(solution)/shard_map/while/body/eval_jaxpr/ppermute | solution.py:13
  168.9 6.4 %collective-permute-start.2 = (f32[128,128]{1,0:T(8,128)S(1)}, f32[128,128]{1,0:T(8,128)S(1)}, u32[]{:S(2)}, u32[]{:S(2)}) collective-permute-start(f32[128,128]{1,0:T(8,128)S(1)} %fusion.123), channel_id=1, source_target_pairs={{0,1},{1,2},{2,3},{3,4},{4,5},{5,6},{6,7},{7,8},{8,9},{9,10},{10,1... | collective-permute-start | bytes 196616 | tf_op jit(solution)/shard_map/while/body/eval_jaxpr/ppermute | solution.py:13
  169.2 6.8 %collective-permute-start.3 = (f32[128,128]{1,0:T(8,128)S(1)}, f32[128,128]{1,0:T(8,128)S(1)}, u32[]{:S(2)}, u32[]{:S(2)}) collective-permute-start(f32[128,128]{1,0:T(8,128)S(1)} %convolution_add_fusion.6), channel_id=1, source_target_pairs={{0,1},{1,2},{2,3},{3,4},{4,5},{5,6},{6,7},{7,8},{8,9},{9,10},{10,1... | collective-permute-start | bytes 196616 | tf_op jit(solution)/shard_map/while/body/eval_jaxpr/ppermute | solution.py:13
  176.1 6.0 %collective-permute-start = (bf16[128,128]{1,0:T(8,128)(2,1)S(1)}, bf16[128,128]{1,0:T(8,128)(2,1)S(1)}, u32[]{:S(2)}, u32[]{:S(2)}) collective-permute-start(bf16[128,128]{1,0:T(8,128)(2,1)S(1)} %copy.67), channel_id=1, source_target_pairs={{0,1},{1,2},{2,3},{3,4},{4,5},{5,6},{6,7},{7,8},{8,9},{9,10},{10,1... | collective-permute-start | bytes 98312 | tf_op jit(solution)/shard_map/while/body/eval_jaxpr/ppermute | solution.py:13
  176.1 6.4 %collective-permute-start.1 = (bf16[128,128]{1,0:T(8,128)(2,1)S(1)}, bf16[128,128]{1,0:T(8,128)(2,1)S(1)}, u32[]{:S(2)}, u32[]{:S(2)}) collective-permute-start(bf16[128,128]{1,0:T(8,128)(2,1)S(1)} %copy.68), channel_id=1, source_target_pairs={{0,1},{1,2},{2,3},{3,4},{4,5},{5,6},{6,7},{7,8},{8,9},{9,10},{10,1... | collective-permute-start | bytes 98312 | tf_op jit(solution)/shard_map/while/body/eval_jaxpr/ppermute | solution.py:13
  178.5 6.4 %collective-permute-start.2 = (f32[128,128]{1,0:T(8,128)S(1)}, f32[128,128]{1,0:T(8,128)S(1)}, u32[]{:S(2)}, u32[]{:S(2)}) collective-permute-start(f32[128,128]{1,0:T(8,128)S(1)} %fusion.123), channel_id=1, source_target_pairs={{0,1},{1,2},{2,3},{3,4},{4,5},{5,6},{6,7},{7,8},{8,9},{9,10},{10,1... | collective-permute-start | bytes 196616 | tf_op jit(solution)/shard_map/while/body/eval_jaxpr/ppermute | solution.py:13
  178.8 6.8 %collective-permute-start.3 = (f32[128,128]{1,0:T(8,128)S(1)}, f32[128,128]{1,0:T(8,128)S(1)}, u32[]{:S(2)}, u32[]{:S(2)}) collective-permute-start(f32[128,128]{1,0:T(8,128)S(1)} %convolution_add_fusion.6), channel_id=1, source_target_pairs={{0,1},{1,2},{2,3},{3,4},{4,5},{5,6},{6,7},{7,8},{8,9},{9,10},{10,1... | collective-permute-start | bytes 196616 | tf_op jit(solution)/shard_map/while/body/eval_jaxpr/ppermute | solution.py:13
  185.6 6.0 %collective-permute-start = (bf16[128,128]{1,0:T(8,128)(2,1)S(1)}, bf16[128,128]{1,0:T(8,128)(2,1)S(1)}, u32[]{:S(2)}, u32[]{:S(2)}) collective-permute-start(bf16[128,128]{1,0:T(8,128)(2,1)S(1)} %copy.67), channel_id=1, source_target_pairs={{0,1},{1,2},{2,3},{3,4},{4,5},{5,6},{6,7},{7,8},{8,9},{9,10},{10,1... | collective-permute-start | bytes 98312 | tf_op jit(solution)/shard_map/while/body/eval_jaxpr/ppermute | solution.py:13
  185.6 6.4 %collective-permute-start.1 = (bf16[128,128]{1,0:T(8,128)(2,1)S(1)}, bf16[128,128]{1,0:T(8,128)(2,1)S(1)}, u32[]{:S(2)}, u32[]{:S(2)}) collective-permute-start(bf16[128,128]{1,0:T(8,128)(2,1)S(1)} %copy.68), channel_id=1, source_target_pairs={{0,1},{1,2},{2,3},{3,4},{4,5},{5,6},{6,7},{7,8},{8,9},{9,10},{10,1... | collective-permute-start | bytes 98312 | tf_op jit(solution)/shard_map/while/body/eval_jaxpr/ppermute | solution.py:13
  188.0 6.4 %collective-permute-start.2 = (f32[128,128]{1,0:T(8,128)S(1)}, f32[128,128]{1,0:T(8,128)S(1)}, u32[]{:S(2)}, u32[]{:S(2)}) collective-permute-start(f32[128,128]{1,0:T(8,128)S(1)} %fusion.123), channel_id=1, source_target_pairs={{0,1},{1,2},{2,3},{3,4},{4,5},{5,6},{6,7},{7,8},{8,9},{9,10},{10,1... | collective-permute-start | bytes 196616 | tf_op jit(solution)/shard_map/while/body/eval_jaxpr/ppermute | solution.py:13
  188.3 6.8 %collective-permute-start.3 = (f32[128,128]{1,0:T(8,128)S(1)}, f32[128,128]{1,0:T(8,128)S(1)}, u32[]{:S(2)}, u32[]{:S(2)}) collective-permute-start(f32[128,128]{1,0:T(8,128)S(1)} %convolution_add_fusion.6), channel_id=1, source_target_pairs={{0,1},{1,2},{2,3},{3,4},{4,5},{5,6},{6,7},{7,8},{8,9},{9,10},{10,1... | collective-permute-start | bytes 196616 | tf_op jit(solution)/shard_map/while/body/eval_jaxpr/ppermute | solution.py:13
  195.2 6.0 %collective-permute-start = (bf16[128,128]{1,0:T(8,128)(2,1)S(1)}, bf16[128,128]{1,0:T(8,128)(2,1)S(1)}, u32[]{:S(2)}, u32[]{:S(2)}) collective-permute-start(bf16[128,128]{1,0:T(8,128)(2,1)S(1)} %copy.67), channel_id=1, source_target_pairs={{0,1},{1,2},{2,3},{3,4},{4,5},{5,6},{6,7},{7,8},{8,9},{9,10},{10,1... | collective-permute-start | bytes 98312 | tf_op jit(solution)/shard_map/while/body/eval_jaxpr/ppermute | solution.py:13
  195.2 6.4 %collective-permute-start.1 = (bf16[128,128]{1,0:T(8,128)(2,1)S(1)}, bf16[128,128]{1,0:T(8,128)(2,1)S(1)}, u32[]{:S(2)}, u32[]{:S(2)}) collective-permute-start(bf16[128,128]{1,0:T(8,128)(2,1)S(1)} %copy.68), channel_id=1, source_target_pairs={{0,1},{1,2},{2,3},{3,4},{4,5},{5,6},{6,7},{7,8},{8,9},{9,10},{10,1... | collective-permute-start | bytes 98312 | tf_op jit(solution)/shard_map/while/body/eval_jaxpr/ppermute | solution.py:13
  197.5 6.4 %collective-permute-start.2 = (f32[128,128]{1,0:T(8,128)S(1)}, f32[128,128]{1,0:T(8,128)S(1)}, u32[]{:S(2)}, u32[]{:S(2)}) collective-permute-start(f32[128,128]{1,0:T(8,128)S(1)} %fusion.123), channel_id=1, source_target_pairs={{0,1},{1,2},{2,3},{3,4},{4,5},{5,6},{6,7},{7,8},{8,9},{9,10},{10,1... | collective-permute-start | bytes 196616 | tf_op jit(solution)/shard_map/while/body/eval_jaxpr/ppermute | solution.py:13
  197.8 6.8 %collective-permute-start.3 = (f32[128,128]{1,0:T(8,128)S(1)}, f32[128,128]{1,0:T(8,128)S(1)}, u32[]{:S(2)}, u32[]{:S(2)}) collective-permute-start(f32[128,128]{1,0:T(8,128)S(1)} %convolution_add_fusion.6), channel_id=1, source_target_pairs={{0,1},{1,2},{2,3},{3,4},{4,5},{5,6},{6,7},{7,8},{8,9},{9,10},{10,1... | collective-permute-start | bytes 196616 | tf_op jit(solution)/shard_map/while/body/eval_jaxpr/ppermute | solution.py:13
  204.7 6.0 %collective-permute-start = (bf16[128,128]{1,0:T(8,128)(2,1)S(1)}, bf16[128,128]{1,0:T(8,128)(2,1)S(1)}, u32[]{:S(2)}, u32[]{:S(2)}) collective-permute-start(bf16[128,128]{1,0:T(8,128)(2,1)S(1)} %copy.67), channel_id=1, source_target_pairs={{0,1},{1,2},{2,3},{3,4},{4,5},{5,6},{6,7},{7,8},{8,9},{9,10},{10,1... | collective-permute-start | bytes 98312 | tf_op jit(solution)/shard_map/while/body/eval_jaxpr/ppermute | solution.py:13
  204.7 6.4 %collective-permute-start.1 = (bf16[128,128]{1,0:T(8,128)(2,1)S(1)}, bf16[128,128]{1,0:T(8,128)(2,1)S(1)}, u32[]{:S(2)}, u32[]{:S(2)}) collective-permute-start(bf16[128,128]{1,0:T(8,128)(2,1)S(1)} %copy.68), channel_id=1, source_target_pairs={{0,1},{1,2},{2,3},{3,4},{4,5},{5,6},{6,7},{7,8},{8,9},{9,10},{10,1... | collective-permute-start | bytes 98312 | tf_op jit(solution)/shard_map/while/body/eval_jaxpr/ppermute | solution.py:13
  207.1 6.4 %collective-permute-start.2 = (f32[128,128]{1,0:T(8,128)S(1)}, f32[128,128]{1,0:T(8,128)S(1)}, u32[]{:S(2)}, u32[]{:S(2)}) collective-permute-start(f32[128,128]{1,0:T(8,128)S(1)} %fusion.123), channel_id=1, source_target_pairs={{0,1},{1,2},{2,3},{3,4},{4,5},{5,6},{6,7},{7,8},{8,9},{9,10},{10,1... | collective-permute-start | bytes 196616 | tf_op jit(solution)/shard_map/while/body/eval_jaxpr/ppermute | solution.py:13
  207.4 6.8 %collective-permute-start.3 = (f32[128,128]{1,0:T(8,128)S(1)}, f32[128,128]{1,0:T(8,128)S(1)}, u32[]{:S(2)}, u32[]{:S(2)}) collective-permute-start(f32[128,128]{1,0:T(8,128)S(1)} %convolution_add_fusion.6), channel_id=1, source_target_pairs={{0,1},{1,2},{2,3},{3,4},{4,5},{5,6},{6,7},{7,8},{8,9},{9,10},{10,1... | collective-permute-start | bytes 196616 | tf_op jit(solution)/shard_map/while/body/eval_jaxpr/ppermute | solution.py:13
  214.7 6.4 %collective-permute-start.5 = (f32[128,128]{1,0:T(8,128)S(1)}, f32[128,128]{1,0:T(8,128)S(1)}, u32[]{:S(2)}, u32[]{:S(2)}) collective-permute-start(f32[128,128]{1,0:T(8,128)S(1)} %convolution_add_fusion.2), channel_id=1, source_target_pairs={{0,1},{1,2},{2,3},{3,4},{4,5},{5,6},{6,7},{7,8},{8,9},{9,10},{10,1... | collective-permute-start | bytes 196616 | tf_op jit(solution)/shard_map/ppermute | solution.py:13
  215.1 6.7 %collective-permute-start.4 = (f32[128,128]{1,0:T(8,128)S(1)}, f32[128,128]{1,0:T(8,128)S(1)}, u32[]{:S(2)}, u32[]{:S(2)}) collective-permute-start(f32[128,128]{1,0:T(8,128)S(1)} %fusion.45), channel_id=1, source_target_pairs={{0,1},{1,2},{2,3},{3,4},{4,5},{5,6},{6,7},{7,8},{8,9},{9,10},{10,1... | collective-permute-start | bytes 196616 | tf_op jit(solution)/shard_map/ppermute | solution.py:13
  (3 other events, 2.4 us)
Sparse Core Ops, SparseCore 0:
  10.8 40.6 all-gather.1
